TPU v7x, 128 devices: a whole 4x4x4 slice. The times are simulated.
128 devices in a mesh: row: 8 (over x, y_lo), col: 16 (over z, y_hi, core).
Axes of the slice: x: 4, y: 4 (y_hi: 2, y_lo: 2; y = y_hi * 2 + y_lo), z: 4, core: 2. Of those that a mesh axis runs over, the one named last changes fastest.
Arguments:
- pair: bfloat16 [512, 512, 128], P('row', 'col'), may hold values from -6 to 6
- ln_in: float32 [2, 128], replicated, may hold values from 0.5 to 1.5
- w_left: bfloat16 [2, 128, 256], replicated, may hold values from -0.5 to 0.5
- w_right: bfloat16 [2, 128, 256], replicated, may hold values from -0.5 to 0.5
- w_gate: bfloat16 [2, 128, 128], replicated, may hold values from -0.5 to 0.5
- ln_out: float32 [2, 128], replicated, may hold values from 0.5 to 1.5
- w_out: bfloat16 [2, 128, 128], replicated, may hold values from -0.5 to 0.5
Outputs:
- updated: bfloat16 [512, 512, 128], P('row', 'col')
All inputs are finite; a program needn't handle non-finite values.
Results may differ from a plain program's by a relative error of at most 0.022.
Values may be sent and summed in bfloat16 or wider, within the bound.
A program may use at most 128 MiB of HBM per device.

v0:
```python
import jax
import jax.numpy as jnp
from jax import lax
from jax.sharding import PartitionSpec as P


def layer_norm(values, gain):
    mean = jnp.mean(values, axis=-1, keepdims=True)
    centred = values - mean
    spread = jnp.mean(centred * centred, axis=-1, keepdims=True)
    return centred * lax.rsqrt(spread + 1e-05) * gain


def project(tile, gain, w_left, w_right, w_gate):
    normed = layer_norm(tile.astype(jnp.float32), gain).astype(jnp.bfloat16)
    hidden = w_left.shape[1] // 2
    pl = jnp.dot(normed, w_left, preferred_element_type=jnp.float32)
    pr = jnp.dot(normed, w_right, preferred_element_type=jnp.float32)
    left = (jax.nn.sigmoid(pl[..., :hidden]) * pl[..., hidden:]).astype(jnp.bfloat16)
    right = (jax.nn.sigmoid(pr[..., :hidden]) * pr[..., hidden:]).astype(jnp.bfloat16)
    gate = jax.nn.sigmoid(jnp.dot(normed, w_gate, preferred_element_type=jnp.float32))
    return (left, right, gate)


def finish(tile, edges, gate, gain, w_out):
    scaled = layer_norm(edges, gain).astype(jnp.bfloat16)
    update = jnp.dot(scaled, w_out, preferred_element_type=jnp.float32)
    return (tile.astype(jnp.float32) + gate * update).astype(jnp.bfloat16)


def local(pair, ln_in, w_left, w_right, w_gate, ln_out, w_out):
    left, right, gate = project(pair, ln_in[0], w_left[0], w_right[0], w_gate[0])
    right_all = lax.all_gather(right, "row", axis=0, tiled=True)
    picked = right_all
    summed = lax.psum_scatter(
        jnp.einsum("jkh,ikh->jih", picked, left, preferred_element_type=jnp.float32).astype(
            jnp.bfloat16
        ),
        "col",
        scatter_dimension=0,
        tiled=True,
    ).astype(jnp.float32)
    edges = jnp.transpose(summed, (1, 0, 2))
    middle = finish(pair, edges, gate, ln_out[0], w_out[0])
    left, right, gate = project(middle, ln_in[1], w_left[1], w_right[1], w_gate[1])
    left_all = lax.all_gather(left, "col", axis=1, tiled=True)
    picked = left_all
    edges = lax.psum_scatter(
        jnp.einsum("kih,kjh->ijh", picked, right, preferred_element_type=jnp.float32).astype(
            jnp.bfloat16
        ),
        "row",
        scatter_dimension=0,
        tiled=True,
    ).astype(jnp.float32)
    return finish(middle, edges, gate, ln_out[1], w_out[1])


def solution(mesh):
    return jax.shard_map(
        local,
        mesh=mesh,
        in_specs=(P("row", "col", None), P(), P(), P(), P(), P(), P()),
        out_specs=P("row", "col", None),
        check_vma=False,
    )
```

profile of v0, /device:TPU:1, one launch (start us, length us, event | category | flops | bytes accessed | tf_op | source)
XLA Modules:
  0.0 477.2 jit_solution(2881064755426946546)
XLA Ops:
  6.5 1.4 convert_reduce_fusion.1
  8.2 1.7 fusion.19
  10.0 0.8 slice_bitcast_fusion.1
  10.8 1.8 fusion.53
  12.6 1.1 fusion.33
  13.7 0.7 fusion.55
  14.7 1.7 copy.63
  16.4 90.3 %all-gather.3.cloned.1.call-done = bf16[512,32,128]{2,1,0:T(8,128)(2,1)} async-done(((bf16[64,32,128]{2,1,0:T(8,128)(2,1)}), bf16[512,32,128]{2,1,0:T(8,128)(2,1)}) %all-gather.3.cloned.1.call-update) | async-done | bytes 4194320 | tf_op jit(solution)/shard_map/all_gather | solution.py:33
  106.7 8.5 %copy.64 = bf16[512,32,128]{0,1,2:T(8,128)(2,1)} copy(bf16[512,32,128]{2,1,0:T(8,128)(2,1)} %all-gather.3.cloned.1.call-done) | data formatting | bytes 8388608 | tf_op jit(solution)/shard_map/all_gather | solution.py:33
  115.3 7.8 %convert_bitcast_fusion = bf16[512,64,128]{0,1,2:T(8,128)(2,1)} fusion(bf16[64,32,128]{0,1,2:T(8,128)(2,1)S(1)} %copy.63, bf16[512,32,128]{0,1,2:T(8,128)(2,1)} %copy.64), kind=kOutput, calls=%fused_computation | convolution fusion | flops 272629760 | bytes 13107200 | tf_op jit(solution)/shard_map/jkh,ikh->jih/dot_general | solution.py:36
  123.1 13.7 %copy.65 = bf16[512,64,128]{2,1,0:T(8,128)(2,1)} copy(bf16[512,64,128]{0,1,2:T(8,128)(2,1)} %convert_bitcast_fusion) | data formatting | bytes 16777216 | tf_op jit(solution)/shard_map/convert_element_type | solution.py:36
  137.0 0.4 copy-done.4
  137.4 103.4 %reduce-scatter.3.cloned.1.call-done = bf16[32,64,128]{2,1,0:T(8,128)(2,1)} async-done(((bf16[512,64,128]{2,1,0:T(8,128)(2,1)}), bf16[32,64,128]{2,1,0:T(8,128)(2,1)}) %reduce-scatter.3.cloned.1.call-update) | async-done | bytes 524304 | tf_op jit(solution)/shard_map/reduce_scatter | solution.py:35
  240.9 1.4 bitcast_reduce_fusion
  242.3 1.7 fusion.43
  244.0 1.6 fusion.45
  245.6 0.4 fusion.48
  246.1 1.2 convert_reduce_fusion
  247.4 0.6 fusion.16
  248.2 0.7 fusion.58
  248.9 1.1 fusion.25
  250.1 0.7 fusion.60
  251.1 1.7 copy.71
  252.8 74.8 %all-gather.5.cloned.1.call-done = bf16[64,512,128]{2,1,0:T(8,128)(2,1)} async-done(((bf16[64,32,128]{2,1,0:T(8,128)(2,1)}), bf16[64,512,128]{2,1,0:T(8,128)(2,1)}) %all-gather.5.cloned.1.call-update) | async-done | bytes 8388624 | tf_op jit(solution)/shard_map/all_gather | solution.py:46
  327.7 29.1 %copy.72 = bf16[64,512,128]{0,1,2:T(8,128)(2,1)} copy(bf16[64,512,128]{2,1,0:T(8,128)(2,1)} %all-gather.5.cloned.1.call-done) | data formatting | bytes 16777216 | tf_op jit(solution)/shard_map/all_gather | solution.py:46
  356.8 10.5 %convert_bitcast_fusion.1 = bf16[512,32,128]{0,1,2:T(8,128)(2,1)} fusion(bf16[64,32,128]{0,1,2:T(8,128)(2,1)S(1)} %copy.71, bf16[64,512,128]{0,1,2:T(8,128)(2,1)} %copy.72), kind=kOutput, calls=%fused_computation.1 | convolution fusion | flops 270532608 | bytes 13107200 | tf_op jit(solution)/shard_map/kih,kjh->ijh/dot_general | solution.py:49
  367.3 9.1 %copy.73 = bf16[512,32,128]{2,1,0:T(8,128)(2,1)} copy(bf16[512,32,128]{0,1,2:T(8,128)(2,1)} %convert_bitcast_fusion.1) | data formatting | bytes 8388608 | tf_op jit(solution)/shard_map/convert_element_type | solution.py:49
  376.4 87.4 %reduce-scatter.5.cloned.1.call-done = bf16[64,32,128]{2,1,0:T(8,128)(2,1)} async-done(((bf16[512,32,128]{2,1,0:T(8,128)(2,1)}), bf16[64,32,128]{2,1,0:T(8,128)(2,1)}) %reduce-scatter.5.cloned.1.call-update) | async-done | bytes 524304 | tf_op jit(solution)/shard_map/reduce_scatter | solution.py:48
  463.8 1.4 convert_reduce_fusion.2
  465.4 1.7 fusion.22
  467.2 1.8 fusion.46
  469.0 1.7 fusion.9
  (42 shorter events, 1.9 us)
Async XLA Ops:
  6.5 7.2 %copy-start = (bf16[64,32,128]{2,1,0:T(8,128)(2,1)S(1)}, bf16[64,32,128]{2,1,0:T(8,128)(2,1)}, u32[]{:S(2)}) copy-start(bf16[64,32,128]{2,1,0:T(8,128)(2,1)} %param.7) | copy-start | bytes 1572868
  6.5 7.2 %copy-start.1 = (bf16[2,128,256]{2,1,0:T(8,128)(2,1)S(1)}, bf16[2,128,256]{2,1,0:T(8,128)(2,1)}, u32[]{:S(2)}) copy-start(bf16[2,128,256]{2,1,0:T(8,128)(2,1)} %param.9) | copy-start | bytes 393220
  6.5 100.2 %all-gather.3.cloned.1.call-start = ((), (), s32[]{:S(2)}) async-start(), calls=%async_computation.2 | async-start | bytes 4718592 | tf_op jit(solution)/shard_map/all_gather | solution.py:33
  13.7 227.2 %reduce-scatter.3.cloned.1.call-start = ((), (), s32[]{:S(2)}) async-start(), calls=%async_computation.3 | async-start | bytes 8912896 | tf_op jit(solution)/shard_map/reduce_scatter | solution.py:35
  136.8 0.7 copy-start.4
  136.8 108.9 %copy-start.3 = (bf16[2,128,128]{2,1,0:T(8,128)(2,1)S(1)}, bf16[2,128,128]{2,1,0:T(8,128)(2,1)}, u32[]{:S(2)}) copy-start(bf16[2,128,128]{2,1,0:T(8,128)(2,1)} %param.13) | copy-start | bytes 196612
  136.8 109.3 %copy-start.5 = (bf16[2,128,128]{2,1,0:T(8,128)(2,1)S(1)}, bf16[2,128,128]{2,1,0:T(8,128)(2,1)}, u32[]{:S(2)}) copy-start(bf16[2,128,128]{2,1,0:T(8,128)(2,1)} %param.11) | copy-start | bytes 196612
  136.8 190.9 %all-gather.5.cloned.1.call-start = ((), (), s32[]{:S(2)}) async-start(), calls=%async_computation.4 | async-start | bytes 8912896 | tf_op jit(solution)/shard_map/all_gather | solution.py:46
  247.2 2.9 copy-start.2
  250.0 213.8 %reduce-scatter.5.cloned.1.call-start = ((), (), s32[]{:S(2)}) async-start(), calls=%async_computation.5 | async-start | bytes 4718592 | tf_op jit(solution)/shard_map/reduce_scatter | solution.py:48
Sparse Core Ops, SparseCore 0:
  13.8 92.9 all-gather.2
  136.9 103.9 reduce-scatter.2
  250.2 77.4 all-gather.4
  376.5 87.2 reduce-scatter.4
where the time goes:
time: 478 us; the launch traced here: 477 us
  waiting for transfers between devices  356 us (74%)
  local copies, waits for them, and re-layouts  66 us (14%)
  matrix products  27.3 us (6%)
  other arithmetic  14.4 us (3%)
  between operations  13.3 us (3%)
    reduce_scatter x1, waiting for transfers between devices, local(): lax.psum_scatter(jnp.einsum('jkh,ikh->jih', picked, left, preferred_eleme...  103 us
    all_gather x1, waiting for transfers between devices, local(): right_all = lax.all_gather(right, 'row', axis=0, tiled=True)  90.3 us
    reduce_scatter x1, waiting for transfers between devices, local(): lax.psum_scatter(jnp.einsum('kih,kjh->ijh', picked, right, preferred_elem...  87.4 us
    all_gather x1, waiting for transfers between devices, local(): left_all = lax.all_gather(left, 'col', axis=1, tiled=True)  74.8 us
    all_gather x1, local copies, waits for them, and re-layouts, local(): left_all = lax.all_gather(left, 'col', axis=1, tiled=True)  29.1 us
    convert_element_type x1, local copies, waits for them, and re-layouts, local(): jnp.einsum('jkh,ikh->jih', picked, left, preferred_element_type=jnp.float32)  13.7 us
    dot_general x1, matrix products, local(): jnp.einsum('kih,kjh->ijh', picked, right, preferred_element_type=jnp.floa...  10.5 us
  transfers between devices with their start and end apart: 4, of which 4 were waited for; matrix products, arithmetic and copies ran while one was open for 1% of the time, Pallas kernels for 0%

commit v1 on v0

v1 whole, which is shorter than its diff:
```python
import functools

import jax
import jax.numpy as jnp
from jax import lax
from jax.experimental import pallas as pl
from jax.experimental.pallas import tpu as pltpu
from jax.sharding import PartitionSpec as P


MESH = pl.DeviceIdType.MESH
F32, BF16 = jnp.float32, jnp.bfloat16
EPS = 1e-05


def place():
    row, col = lax.axis_index("row"), lax.axis_index("col")
    return row // 2, ((col // 2) % 2) * 2 + row % 2, col // 4, col % 2


def device_at(x, y, z, core):
    return x * 2 + y % 2, z * 4 + (y // 2) * 2 + core


def channel_at(x, y, z, core):
    return (((x + y + z) % 4) * 2 + core) * 16 + y * 4 + z


def norm_rows(values, gain):
    mean = jnp.mean(values, axis=0, keepdims=True)
    centred = values - mean
    spread = jnp.mean(centred * centred, axis=0, keepdims=True)
    return centred * lax.rsqrt(spread + EPS) * gain


def turned(matrix):
    return jnp.transpose(matrix.astype(F32))


def swap_halves(first, second):
    low = jnp.concatenate([first[:, :64], second[:, :64]], axis=1)
    high = jnp.concatenate([first[:, 64:], second[:, 64:]], axis=1)
    return low, high


def kernel(
    pair_ref, ln_in_ref, w_left_ref, w_right_ref, w_gate_ref, ln_out_ref, w_out_ref, out_ref,
    flat, tile, normed, gate, spread_buf, w_proj, w_turn, mat_l, mat_r,
    send_l, send_r, send_e, recv_l, recv_r, recv_e, send_sem, recv_sem,
):
    x, y, z, core = place()
    me_row, me_col = lax.axis_index("row"), lax.axis_index("col")
    me = me_row * 16 + me_col
    my_channel = channel_at(x, y, z, core)

    def partner(step, e):
        da, db = 3 - step // 2, 1 - step % 2
        dy, dz = 3 - e // 4, 3 - e % 4
        py, pz = (y + dy) % 4, (z + dz) % 4
        px = (x + da - dy - dz + 8) % 4
        return px, py, pz, (core + db) % 2

    barrier = pltpu.get_barrier_semaphore()

    def greet(n, carry):
        pr, pc = device_at(*partner(n // 16, n % 16))
        pl.semaphore_signal(barrier, inc=1, device_id=(pr, pc), device_id_type=MESH)
        return carry

    lax.fori_loop(0, 127, greet, 0)

    flat[...] = pair_ref[...].reshape(2048, 128).astype(F32)
    for u in range(2):
        left, right = turned(w_left_ref[u]).astype(BF16), turned(w_right_ref[u]).astype(BF16)
        for j in range(8):
            w_proj[u, 0, j, 0:16] = left[16 * j : 16 * j + 16]
            w_proj[u, 0, j, 16:32] = left[128 + 16 * j : 144 + 16 * j]
            w_proj[u, 1, j, 0:16] = right[16 * j : 16 * j + 16]
            w_proj[u, 1, j, 16:32] = right[128 + 16 * j : 144 + 16 * j]
        w_turn[u, 0] = turned(w_gate_ref[u]).astype(BF16)
        w_turn[u, 1] = turned(w_out_ref[u]).astype(BF16)

    def gain_of(ref, u):
        return jnp.transpose(jnp.broadcast_to(ref[u : u + 1, :], (128, 128)))

    gain_in = gain_of(ln_in_ref, 0)
    for s in range(16):
        block = jnp.concatenate(
            [flat[pl.ds(s, 64, stride=32), :], flat[pl.ds(16 + s, 64, stride=32), :]], axis=0
        )
        block = jnp.transpose(block)
        tile[:, s * 128 : s * 128 + 128] = block.astype(BF16)
        normed[:, s * 128 : s * 128 + 128] = norm_rows(block, gain_in).astype(BF16)

    pl.semaphore_wait(barrier, 127)

    def start(src, dst, slot, u, n, step, e, peer):
        pr, pc = device_at(*peer)

        @pl.when((step < 7) | (e < 15))
        def _():
            pltpu.make_async_remote_copy(
                src_ref=src,
                dst_ref=dst,
                send_sem=send_sem.at[u, n],
                recv_sem=recv_sem.at[u, n],
                device_id=(pr, pc),
                device_id_type=MESH,
            ).start()

        @pl.when((step == 7) & (e == 15))
        def _():
            pltpu.make_async_copy(src, dst, recv_sem.at[u, n]).start()

    for u in range(2):

        def project(side, send, recv, n):
            def step_body(step, carry):
                da, db = 3 - step // 2, 1 - step % 2
                j = ((x + y + z + da) % 4) * 2 + (core + db) % 2
                p = jnp.dot(w_proj[u, side, j], normed[...], preferred_element_type=F32)
                value = jax.nn.sigmoid(p[:16]) * p[16:]
                for s in range(16):
                    spread_buf[pl.ds(s, 16, stride=16), :] = value[:, s * 128 : s * 128 + 128]
                send[u, pl.ds(pl.multiple_of(j * 256, 256), 256), :] = spread_buf[0:256, :].astype(BF16)
                for e in range(16):
                    peer = partner(step, e)
                    there = pl.multiple_of(channel_at(*peer) * 16, 16)
                    here = pl.multiple_of(me * 16, 16)
                    start(
                        send.at[u, pl.ds(there, 16), :], recv.at[u, pl.ds(here, 16), :],
                        None, u, n, step, e, peer,
                    )
                return carry

            lax.fori_loop(0, 8, step_body, 0)

        project(1, send_r, recv_r, 0)
        project(0, send_l, recv_l, 1)

        gate[...] = jax.nn.sigmoid(jnp.dot(w_turn[u, 0], normed[...], preferred_element_type=F32))

        def gather(recv, mat):
            def body(c, carry):
                for m in range(4):
                    first = recv[u, pl.ds(pl.multiple_of((32 * m + c) * 16, 16), 16), :]
                    second = recv[u, pl.ds(pl.multiple_of((32 * m + 16 + c) * 16, 16), 16), :]
                    low, high = swap_halves(first, second)
                    mat[pl.ds(pl.multiple_of(c * 32, 32), 16), m * 128 : m * 128 + 128] = low
                    mat[pl.ds(pl.multiple_of(c * 32 + 16, 16), 16), m * 128 : m * 128 + 128] = high
                return carry

            lax.fori_loop(0, 16, body, 0)

        def arrived(recv, n):
            pltpu.make_async_copy(recv.at[u], recv.at[u], recv_sem.at[u, n]).wait()

        arrived(recv_r, 0)
        gather(recv_r, mat_r)
        if u == 0:
            mat_r[...] = jnp.transpose(mat_r[...].astype(F32)).astype(BF16)
        arrived(recv_l, 1)
        gather(recv_l, mat_l)
        contract = (((1,), (0,)), ((), ())) if u == 0 else (((1,), (1,)), ((), ()))
        for c4 in range(4):
            edges = lax.dot_general(
                mat_r[c4 * 128 : c4 * 128 + 128, :], mat_l[...], contract, preferred_element_type=F32
            ).astype(BF16)
            for c in range(4):
                for m in range(4):
                    low, high = swap_halves(
                        edges[c * 32 : c * 32 + 16, m * 128 : m * 128 + 128],
                        edges[c * 32 + 16 : c * 32 + 32, m * 128 : m * 128 + 128],
                    )
                    at = (32 * m + 4 * c4 + c) * 16
                    send_e[u, at : at + 16, :] = low
                    send_e[u, at + 256 : at + 272, :] = high

        def back(step, carry):
            for e in range(16):
                peer = partner(step, e)
                pr, pc = device_at(*peer)
                there = pl.multiple_of((pr * 16 + pc) * 16, 16)
                here = pl.multiple_of(my_channel * 16, 16)
                start(
                    send_e.at[u, pl.ds(there, 16), :], recv_e.at[u, pl.ds(here, 16), :],
                    None, u, 2, step, e, peer,
                )
            return carry

        lax.fori_loop(0, 8, back, 0)
        gain_out = gain_of(ln_out_ref, u)
        gain_next = gain_of(ln_in_ref, 1)
        arrived(recv_e, 2)
        spread_buf[...] = recv_e[u].astype(F32)
        for s in range(16):
            lanes = slice(s * 128, s * 128 + 128)
            scaled = norm_rows(spread_buf[pl.ds(s, 128, stride=16), :], gain_out).astype(BF16)
            update = jnp.dot(w_turn[u, 1], scaled, preferred_element_type=F32)
            updated = tile[:, lanes].astype(F32) + gate[:, lanes] * update
            if u == 0:
                rounded = updated.astype(BF16)
                tile[:, lanes] = rounded
                normed[:, lanes] = norm_rows(rounded.astype(F32), gain_next).astype(BF16)
            else:
                block = jnp.transpose(updated)
                flat[pl.ds(s, 64, stride=32), :] = block[:64]
                flat[pl.ds(16 + s, 64, stride=32), :] = block[64:]
    out_ref[...] = flat[...].astype(BF16).reshape(64, 32, 128)

    for u in range(2):
        for n, send in enumerate((send_r, send_l, send_e)):
            sent = send.at[u, pl.ds(0, 127 * 16), :]
            pltpu.make_async_copy(sent, sent, send_sem.at[u, n]).wait()


def local(pair, ln_in, w_left, w_right, w_gate, ln_out, w_out):
    tokens = pltpu.VMEM((2, 2048, 128), BF16)
    return pl.pallas_call(
        kernel,
        out_shape=jax.ShapeDtypeStruct((64, 32, 128), BF16),
        in_specs=[pl.BlockSpec(memory_space=pltpu.VMEM)] * 7,
        out_specs=pl.BlockSpec(memory_space=pltpu.VMEM),
        scratch_shapes=[
            pltpu.VMEM((2048, 128), F32),
            pltpu.VMEM((128, 2048), BF16),
            pltpu.VMEM((128, 2048), BF16),
            pltpu.VMEM((128, 2048), F32),
            pltpu.VMEM((2048, 128), F32),
            pltpu.VMEM((2, 2, 8, 32, 128), BF16),
            pltpu.VMEM((2, 2, 128, 128), BF16),
            pltpu.VMEM((512, 512), BF16),
            pltpu.VMEM((512, 512), BF16),
            tokens, tokens, tokens, tokens, tokens, tokens,
            pltpu.SemaphoreType.DMA((2, 3)),
            pltpu.SemaphoreType.DMA((2, 3)),
        ],
        compiler_params=pltpu.CompilerParams(
            collective_id=0, has_side_effects=True, vmem_limit_bytes=48 << 20
        ),
        name="triangle",
    )(pair, ln_in, w_left, w_right, w_gate, ln_out, w_out)


def solution(mesh):
    return jax.shard_map(
        local,
        mesh=mesh,
        in_specs=(P("row", "col", None), P(), P(), P(), P(), P(), P()),
        out_specs=P("row", "col", None),
        check_vma=False,
    )
```

time: 478 us -> 78.9 us (0.17)
  waiting for transfers between devices: 356 us -> 0 us
  Pallas kernels: 0 us -> 71.9 us
  local copies, waits for them, and re-layouts: 66 us -> 6.68 us
  matrix products: 27.3 us -> 0 us
  other arithmetic: 14.4 us -> 0 us
  between operations: 13.3 us -> 0.02 us
    reduce_scatter x2 -> x0, waiting for transfers between devices: 191 us -> none  [the longest x1 103 us: local(): lax.psum_scatter(jnp.einsum('jkh,ikh->jih', picked, left, preferred_eleme...]
    all_gather x2 -> x0, waiting for transfers between devices: 165 us -> none  [the longest x1 90.3 us: local(): right_all = lax.all_gather(right, 'row', axis=0, tiled=True)]
    pallas_call x0 -> x1, Pallas kernels: none -> 71.9 us  [local(): pl.pallas_call(kernel, out_shape=jax.ShapeDtypeStruct((64, 32, 128), BF16...]
    all_gather x2 -> x0, local copies, waits for them, and re-layouts: 37.7 us -> none  [the longest x1 29.1 us: local(): left_all = lax.all_gather(left, 'col', axis=1, tiled=True)]
    dot_general x10 -> x0, matrix products: 27.3 us -> none  [the longest x1 10.5 us: local(): jnp.einsum('kih,kjh->ijh', picked, right, preferred_element_type=jnp.floa...]
    convert_element_type x4 -> x0, local copies, waits for them, and re-layouts: 26.2 us -> none  [the longest x1 13.7 us: local(): jnp.einsum('jkh,ikh->jih', picked, left, preferred_element_type=jnp.float32)]
    reduce_sum x7 -> x0, other arithmetic: 9.92 us -> none  [the longest x4 5.7 us: layer_norm(): spread = jnp.mean(centred * centred, axis=-1, keepdims=True)]
    unnamed x14 -> x15, local copies, waits for them, and re-layouts: 0.57 us -> 6.68 us
  transfers between devices with their start and end apart: 4 -> 0, of which waited for: 4 -> 0; matrix products, arithmetic and copies ran while one was open for 1% -> 0% of each run, Pallas kernels for 0% -> 0%
where the time goes in v1:
time: 78.9 us; the launch traced here: 78.6 us
  Pallas kernels  71.9 us (91%)
  local copies, waits for them, and re-layouts  6.68 us (8%)
    pallas_call x1, Pallas kernels, local(): pl.pallas_call(kernel, out_shape=jax.ShapeDtypeStruct((64, 32, 128), BF16...  71.9 us
    unnamed x15, local copies, waits for them, and re-layouts  6.68 us

profile of v1, /device:TPU:1, one launch (start us, length us, event | category | flops | bytes accessed | tf_op | source)
XLA Modules:
  0.0 78.6 jit_solution(10485891736176594549)
XLA Ops:
  0.0 0.0 copy-start
  0.0 1.0 %copy-done = bf16[64,32,128]{2,1,0:T(8,128)(2,1)S(1)} copy-done((bf16[64,32,128]{2,1,0:T(8,128)(2,1)S(1)}, bf16[64,32,128]{2,1,0:T(8,128)(2,1)}, u32[]{:S(2)}) %copy-start) | copy-done | bytes 524312
  1.0 0.0 copy-start.1
  1.0 0.9 %copy-done.1 = bf16[2,128,256]{2,1,0:T(8,128)(2,1)S(1)} copy-done((bf16[2,128,256]{2,1,0:T(8,128)(2,1)S(1)}, bf16[2,128,256]{2,1,0:T(8,128)(2,1)}, u32[]{:S(2)}) %copy-start.1) | copy-done | bytes 131096
  1.9 0.0 copy-start.2
  1.9 0.9 %copy-done.2 = bf16[2,128,256]{2,1,0:T(8,128)(2,1)S(1)} copy-done((bf16[2,128,256]{2,1,0:T(8,128)(2,1)S(1)}, bf16[2,128,256]{2,1,0:T(8,128)(2,1)}, u32[]{:S(2)}) %copy-start.2) | copy-done | bytes 131096
  2.9 0.0 copy-start.3
  2.9 0.8 %copy-done.3 = bf16[2,128,128]{2,1,0:T(8,128)(2,1)S(1)} copy-done((bf16[2,128,128]{2,1,0:T(8,128)(2,1)S(1)}, bf16[2,128,128]{2,1,0:T(8,128)(2,1)}, u32[]{:S(2)}) %copy-start.3) | copy-done | bytes 65560
  3.7 0.0 copy-start.4
  3.7 0.8 %copy-done.4 = bf16[2,128,128]{2,1,0:T(8,128)(2,1)S(1)} copy-done((bf16[2,128,128]{2,1,0:T(8,128)(2,1)S(1)}, bf16[2,128,128]{2,1,0:T(8,128)(2,1)}, u32[]{:S(2)}) %copy-start.4) | copy-done | bytes 65560
  4.5 0.0 copy-start.5
  4.5 0.7 copy-done.5
  5.2 0.0 copy-start.6
  5.2 0.7 copy-done.6
  5.9 71.9 %triangle.1 = bf16[64,32,128]{2,1,0:T(8,128)(2,1)S(1)} custom-call(bf16[64,32,128]{2,1,0:T(8,128)(2,1)S(1)} %copy-done, f32[2,128]{1,0:T(2,128)S(1)} %copy-done.5, bf16[2,128,256]{2,1,0:T(8,128)(2,1)S(1)} %copy-done.1, bf16[2,128,256]{2,1,0:T(8,128)(2,1)S(1)} %copy-done.2, bf16[2,128,128]{2,1,0:T(8,128)(2,1)S(1)} %copy-done.3, f32[2,128]{1,0:T(2,128)S(1)} %copy-done.6, ...), custom_call_target="tpu_custom_call" | custom-call | tf_op jit(solution)/shard_map/triangle/pallas_call | solution.py:219
  77.8 0.8 %copy.9 = bf16[64,32,128]{2,1,0:T(8,128)(2,1)} copy(bf16[64,32,128]{2,1,0:T(8,128)(2,1)S(1)} %triangle.1) | data formatting | bytes 1048576
Async XLA Ops:
  0.0 1.0 %copy-start = (bf16[64,32,128]{2,1,0:T(8,128)(2,1)S(1)}, bf16[64,32,128]{2,1,0:T(8,128)(2,1)}, u32[]{:S(2)}) copy-start(bf16[64,32,128]{2,1,0:T(8,128)(2,1)} %pair_ref.1) | copy-start | bytes 1572868
  1.0 0.9 %copy-start.1 = (bf16[2,128,256]{2,1,0:T(8,128)(2,1)S(1)}, bf16[2,128,256]{2,1,0:T(8,128)(2,1)}, u32[]{:S(2)}) copy-start(bf16[2,128,256]{2,1,0:T(8,128)(2,1)} %w_left_ref.1) | copy-start | bytes 393220
  1.9 0.9 %copy-start.2 = (bf16[2,128,256]{2,1,0:T(8,128)(2,1)S(1)}, bf16[2,128,256]{2,1,0:T(8,128)(2,1)}, u32[]{:S(2)}) copy-start(bf16[2,128,256]{2,1,0:T(8,128)(2,1)} %w_right_ref.1) | copy-start | bytes 393220
  2.9 0.8 %copy-start.3 = (bf16[2,128,128]{2,1,0:T(8,128)(2,1)S(1)}, bf16[2,128,128]{2,1,0:T(8,128)(2,1)}, u32[]{:S(2)}) copy-start(bf16[2,128,128]{2,1,0:T(8,128)(2,1)} %w_gate_ref.1) | copy-start | bytes 196612
  3.7 0.8 %copy-start.4 = (bf16[2,128,128]{2,1,0:T(8,128)(2,1)S(1)}, bf16[2,128,128]{2,1,0:T(8,128)(2,1)}, u32[]{:S(2)}) copy-start(bf16[2,128,128]{2,1,0:T(8,128)(2,1)} %w_out_ref.1) | copy-start | bytes 196612
  4.5 0.7 copy-start.5
  5.2 0.7 copy-start.6

commit v2 on v1

v2 whole, which is shorter than its diff:
```python
import functools

import jax
import jax.numpy as jnp
from jax import lax
from jax.experimental import pallas as pl
from jax.experimental.pallas import tpu as pltpu
from jax.sharding import PartitionSpec as P


MESH = pl.DeviceIdType.MESH
F32, BF16 = jnp.float32, jnp.bfloat16
EPS = 1e-05
FAR = (2, 1, 3, 0)


def norm_rows(values, gain):
    mean = jnp.mean(values, axis=0, keepdims=True)
    centred = values - mean
    spread = jnp.mean(centred * centred, axis=0, keepdims=True)
    return centred * lax.rsqrt(spread + EPS) * gain


def turned(matrix):
    return jnp.transpose(matrix.astype(F32))


def swap_halves(first, second):
    low = jnp.concatenate([first[:, :64], second[:, :64]], axis=1)
    high = jnp.concatenate([first[:, 64:], second[:, 64:]], axis=1)
    return low, high


def at(index, unit, count=1):
    return pl.ds(pl.multiple_of(index * unit, unit), unit * count)


def kernel(
    pair_hbm, ln_in_hbm, w_left_hbm, w_right_hbm, w_gate_hbm, ln_out_hbm, w_out_hbm, out_ref,
    pair_ref, ln_in_ref, w_left_ref, w_right_ref, w_gate_ref, ln_out_ref, w_out_ref,
    flat, tile, normed, gate, spread_buf, w_proj, w_turn, mat_l, mat_r,
    send_l, send_r, send_e, recv_l, recv_r, recv_e, load_sem, send_sem, recv_sem, edge_sem,
):
    row, col = lax.axis_index("row"), lax.axis_index("col")
    x, y, z, core = row // 2, ((col // 2) % 2) * 2 + row % 2, col // 4, col % 2
    xs = [(x + d) % 4 for d in range(4)]
    ys = [(y + d) % 4 for d in range(4)]
    zs = [(z + d) % 4 for d in range(4)]
    cores = [core, 1 - core]
    my_a = (x + y + z) % 4
    my_channel = (my_a * 2 + core) * 16 + y * 4 + z

    def device_at(px, py, pz, pcore):
        return px * 2 + py % 2, pz * 4 + (py // 2) * 2 + pcore

    loads = []
    pairs = (
        (pair_hbm, pair_ref), (ln_in_hbm, ln_in_ref), (w_right_hbm, w_right_ref), (w_left_hbm, w_left_ref),
        (w_gate_hbm, w_gate_ref), (ln_out_hbm, ln_out_ref), (w_out_hbm, w_out_ref),
    )
    for n, (src, dst) in enumerate(pairs):
        loads.append(pltpu.make_async_copy(src, dst, load_sem.at[n]))
        loads[-1].start()

    barrier = pltpu.get_barrier_semaphore()
    for dx in FAR:
        for dy in FAR:
            for dz in FAR:
                for dc in (1, 0):
                    if dx or dy or dz or dc:
                        pl.semaphore_signal(
                            barrier, inc=1, device_id=device_at(xs[dx], ys[dy], zs[dz], cores[dc]),
                            device_id_type=MESH,
                        )

    def prepare(u, side):
        both = turned((w_left_ref, w_right_ref)[side][u]).astype(BF16)
        for j in range(8):
            w_proj[u, side, j, 0:16] = both[16 * j : 16 * j + 16]
            w_proj[u, side, j, 16:32] = both[128 + 16 * j : 144 + 16 * j]

    def gain_of(ref, u):
        return jnp.transpose(jnp.broadcast_to(ref[u : u + 1, :], (128, 128)))

    loads[0].wait()
    loads[1].wait()
    flat[...] = pair_ref[...].reshape(2048, 128).astype(F32)
    gain_in = gain_of(ln_in_ref, 0)
    for s in range(16):
        block = jnp.concatenate(
            [flat[pl.ds(s, 64, stride=32), :], flat[pl.ds(16 + s, 64, stride=32), :]], axis=0
        )
        block = jnp.transpose(block)
        tile[:, s * 128 : s * 128 + 128] = block.astype(BF16)
        normed[:, s * 128 : s * 128 + 128] = norm_rows(block, gain_in).astype(BF16)
    loads[2].wait()
    prepare(0, 1)
    pl.semaphore_wait(barrier, 127)

    def send_to(src, dst, out_sem, in_sem, peer, may_be_me=None):
        def remote():
            pltpu.make_async_remote_copy(
                src_ref=src, dst_ref=dst, send_sem=out_sem, recv_sem=in_sem,
                device_id=device_at(*peer), device_id_type=MESH,
            ).start()

        if may_be_me is None:
            remote()
        else:
            pl.when(jnp.logical_not(may_be_me))(remote)
            pl.when(may_be_me)(lambda: pltpu.make_async_copy(src, dst, in_sem).start())

    for u in range(2):
        plane = (x, z)[u]
        slot = (row * 16 + col, col * 8 + row)[u]

        def project(side, order, send, recv):
            def step_body(step, carry):
                t, db = step // 2, 1 - step % 2
                a = (plane + t) % 4
                pcore = (core + db) % 2
                j = a * 2 + pcore
                p = jnp.dot(w_proj[u, side, j], normed[...], preferred_element_type=F32)
                value = jax.nn.sigmoid(p[:16]) * p[16:]
                for s in range(16):
                    spread_buf[pl.ds(s, 16, stride=16), :] = value[:, s * 128 : s * 128 + 128]
                send[u, at(j, 256), :] = spread_buf[0:256, :].astype(BF16)
                for dy in FAR:
                    for dz in FAR:
                        peer = ((a - ys[dy] - zs[dz] + 8) % 4, ys[dy], zs[dz], pcore)
                        there = j * 16 + ys[dy] * 4 + zs[dz]
                        send_to(
                            send.at[u, at(there, 16), :], recv.at[u, at(slot, 16), :],
                            send_sem.at[u, order], recv_sem.at[u, order, t], peer,
                            None if dy or dz else (a == my_a) & (db == 0),
                        )
                return carry

            lax.fori_loop(0, 8, step_body, 0)

        def arrived(recv, sem, count):
            some = recv.at[u, pl.ds(0, 16 * count), :]
            pltpu.make_async_copy(some, some, sem).wait()

        def gather(recv, mat, g):
            if u == 0:
                for c in range(16):
                    low, high = swap_halves(
                        recv[u, at(32 * g + c, 16), :], recv[u, at(32 * g + 16 + c, 16), :]
                    )
                    mat[c * 32 : c * 32 + 16, at(g, 128)] = low
                    mat[c * 32 + 16 : c * 32 + 32, at(g, 128)] = high
            else:
                for c in range(4):
                    for m in range(4):
                        slots = recv[u, at(32 * g + 8 * c + 2 * m, 16, 2), :]
                        low, high = swap_halves(slots[:16], slots[16:])
                        mat[at(8 * g + 2 * c, 16), m * 128 : m * 128 + 128] = low
                        mat[at(8 * g + 2 * c + 1, 16), m * 128 : m * 128 + 128] = high

        if u == 0:
            sides = ((1, send_r, recv_r, mat_r), (0, send_l, recv_l, mat_l))
        else:
            sides = ((0, send_l, recv_l, mat_l), (1, send_r, recv_r, mat_r))
        project(sides[0][0], 0, sides[0][1], sides[0][2])
        if u == 0:
            loads[3].wait()
            prepare(0, 0)
        project(sides[1][0], 1, sides[1][1], sides[1][2])

        if u == 0:
            prepare(1, 0)
            prepare(1, 1)
            for n in (4, 5, 6):
                loads[n].wait()
            for v in range(2):
                w_turn[v, 0] = turned(w_gate_ref[v]).astype(BF16)
                w_turn[v, 1] = turned(w_out_ref[v]).astype(BF16)
        gate[...] = jax.nn.sigmoid(jnp.dot(w_turn[u, 0], normed[...], preferred_element_type=F32))

        _, _, recv, mat = sides[0]

        def first_body(t, carry):
            arrived(recv, recv_sem.at[u, 0, t], 32)
            gather(recv, mat, (my_a - t + 4) % 4)
            return carry

        lax.fori_loop(0, 4, first_body, 0)
        if u == 0:
            mat_r[...] = jnp.transpose(mat_r[...].astype(F32)).astype(BF16)

        _, _, recv, mat = sides[1]

        def second_body(t, carry):
            g = (my_a - t + 4) % 4
            arrived(recv, recv_sem.at[u, 1, t], 32)
            gather(recv, mat, g)
            if u == 0:
                edges = jnp.dot(mat_r[...], mat_l[:, at(g, 128)], preferred_element_type=F32).astype(BF16)
                for c in range(16):
                    low, high = swap_halves(
                        edges[c * 32 : c * 32 + 16], edges[c * 32 + 16 : c * 32 + 32]
                    )
                    send_e[u, at(32 * g + c, 16), :] = low
                    send_e[u, at(32 * g + 16 + c, 16), :] = high
            else:
                edges = lax.dot_general(
                    mat_r[at(g, 128), :], mat_l[...], (((1,), (1,)), ((), ())), preferred_element_type=F32
                ).astype(BF16)
                for c in range(4):
                    for m in range(4):
                        lanes = slice(m * 128, m * 128 + 128)
                        low, high = swap_halves(
                            edges[c * 32 : c * 32 + 16, lanes], edges[c * 32 + 16 : c * 32 + 32, lanes]
                        )
                        send_e[u, at(32 * g + 8 * c + 2 * m, 16), :] = low
                        send_e[u, at(32 * g + 8 * c + 2 * m + 1, 16), :] = high
            for d in FAR:
                for dy in FAR:
                    for dc in (1, 0):
                        peer = (g, ys[dy], zs[d], cores[dc]) if u == 0 else (xs[d], ys[dy], g, cores[dc])
                        pr, pc = device_at(*peer)
                        there = (pr * 16 + pc, pc * 8 + pr)[u]
                        send_to(
                            send_e.at[u, at(there, 16), :], recv_e.at[u, at(my_channel, 16), :],
                            send_sem.at[u, 2], edge_sem.at[u], peer,
                            None if d or dy or dc else g == plane,
                        )
            return carry

        lax.fori_loop(0, 4, second_body, 0)

        gain_out = gain_of(ln_out_ref, u)
        gain_next = gain_of(ln_in_ref, 1)
        arrived(recv_e, edge_sem.at[u], 128)
        spread_buf[...] = recv_e[u].astype(F32)
        for s in range(16):
            lanes = slice(s * 128, s * 128 + 128)
            scaled = norm_rows(spread_buf[pl.ds(s, 128, stride=16), :], gain_out).astype(BF16)
            update = jnp.dot(w_turn[u, 1], scaled, preferred_element_type=F32)
            updated = tile[:, lanes].astype(F32) + gate[:, lanes] * update
            if u == 0:
                rounded = updated.astype(BF16)
                tile[:, lanes] = rounded
                normed[:, lanes] = norm_rows(rounded.astype(F32), gain_next).astype(BF16)
            else:
                block = jnp.transpose(updated)
                flat[pl.ds(s, 64, stride=32), :] = block[:64]
                flat[pl.ds(16 + s, 64, stride=32), :] = block[64:]
    out_ref[...] = flat[...].astype(BF16).reshape(64, 32, 128)

    for u in range(2):
        for n, send in enumerate((send_r, send_l, send_e)):
            sent = send.at[u, pl.ds(0, 127 * 16), :]
            pltpu.make_async_copy(sent, sent, send_sem.at[u, n]).wait()


def local(*args):
    tokens = pltpu.VMEM((2, 2048, 128), BF16)
    return pl.pallas_call(
        kernel,
        out_shape=jax.ShapeDtypeStruct((64, 32, 128), BF16),
        in_specs=[pl.BlockSpec(memory_space=pl.ANY)] * 7,
        out_specs=pl.BlockSpec(memory_space=pltpu.VMEM),
        scratch_shapes=[pltpu.VMEM(arg.shape, arg.dtype) for arg in args]
        + [
            pltpu.VMEM((2048, 128), F32),
            pltpu.VMEM((128, 2048), BF16),
            pltpu.VMEM((128, 2048), BF16),
            pltpu.VMEM((128, 2048), F32),
            pltpu.VMEM((2048, 128), F32),
            pltpu.VMEM((2, 2, 8, 32, 128), BF16),
            pltpu.VMEM((2, 2, 128, 128), BF16),
            pltpu.VMEM((512, 512), BF16),
            pltpu.VMEM((512, 512), BF16),
            tokens, tokens, tokens, tokens, tokens, tokens,
            pltpu.SemaphoreType.DMA((7,)),
            pltpu.SemaphoreType.DMA((2, 3)),
            pltpu.SemaphoreType.DMA((2, 2, 4)),
            pltpu.SemaphoreType.DMA((2,)),
        ],
        compiler_params=pltpu.CompilerParams(
            collective_id=0, has_side_effects=True, vmem_limit_bytes=48 << 20
        ),
        name="triangle",
    )(*args)


def solution(mesh):
    return jax.shard_map(
        local,
        mesh=mesh,
        in_specs=(P("row", "col", None), P(), P(), P(), P(), P(), P()),
        out_specs=P("row", "col", None),
        check_vma=False,
    )
```

time: 78.9 us -> 68.6 us (0.87)
  Pallas kernels: 71.9 us -> 61.6 us
    pallas_call x1, Pallas kernels: 71.9 us -> 61.6 us  [local(): pl.pallas_call(kernel, out_shape=jax.ShapeDtypeStruct((64, 32, 128), BF16...]
where the time goes in v2:
time: 68.6 us; the launch traced here: 68.3 us
  Pallas kernels  61.6 us (90%)
  local copies, waits for them, and re-layouts  6.68 us (10%)
    pallas_call x1, Pallas kernels, local(): pl.pallas_call(kernel, out_shape=jax.ShapeDtypeStruct((64, 32, 128), BF16...  61.6 us
    unnamed x15, local copies, waits for them, and re-layouts  6.68 us

profile of v2, /device:TPU:1, one launch (start us, length us, event | category | flops | bytes accessed | tf_op | source)
XLA Modules:
  0.0 68.3 jit_solution(1546574219457575897)
XLA Ops:
  0.0 0.0 copy-start
  0.0 1.0 %copy-done = bf16[64,32,128]{2,1,0:T(8,128)(2,1)S(1)} copy-done((bf16[64,32,128]{2,1,0:T(8,128)(2,1)S(1)}, bf16[64,32,128]{2,1,0:T(8,128)(2,1)}, u32[]{:S(2)}) %copy-start) | copy-done | bytes 524312
  1.0 0.0 copy-start.1
  1.0 0.9 %copy-done.1 = bf16[2,128,256]{2,1,0:T(8,128)(2,1)S(1)} copy-done((bf16[2,128,256]{2,1,0:T(8,128)(2,1)S(1)}, bf16[2,128,256]{2,1,0:T(8,128)(2,1)}, u32[]{:S(2)}) %copy-start.1) | copy-done | bytes 131096
  1.9 0.0 copy-start.2
  1.9 0.9 %copy-done.2 = bf16[2,128,256]{2,1,0:T(8,128)(2,1)S(1)} copy-done((bf16[2,128,256]{2,1,0:T(8,128)(2,1)S(1)}, bf16[2,128,256]{2,1,0:T(8,128)(2,1)}, u32[]{:S(2)}) %copy-start.2) | copy-done | bytes 131096
  2.9 0.0 copy-start.3
  2.9 0.8 %copy-done.3 = bf16[2,128,128]{2,1,0:T(8,128)(2,1)S(1)} copy-done((bf16[2,128,128]{2,1,0:T(8,128)(2,1)S(1)}, bf16[2,128,128]{2,1,0:T(8,128)(2,1)}, u32[]{:S(2)}) %copy-start.3) | copy-done | bytes 65560
  3.7 0.0 copy-start.4
  3.7 0.8 %copy-done.4 = bf16[2,128,128]{2,1,0:T(8,128)(2,1)S(1)} copy-done((bf16[2,128,128]{2,1,0:T(8,128)(2,1)S(1)}, bf16[2,128,128]{2,1,0:T(8,128)(2,1)}, u32[]{:S(2)}) %copy-start.4) | copy-done | bytes 65560
  4.5 0.0 copy-start.5
  4.5 0.7 copy-done.5
  5.2 0.0 copy-start.6
  5.2 0.7 copy-done.6
  5.9 61.6 %triangle.1 = bf16[64,32,128]{2,1,0:T(8,128)(2,1)S(1)} custom-call(bf16[64,32,128]{2,1,0:T(8,128)(2,1)S(1)} %copy-done, f32[2,128]{1,0:T(2,128)S(1)} %copy-done.5, bf16[2,128,256]{2,1,0:T(8,128)(2,1)S(1)} %copy-done.1, bf16[2,128,256]{2,1,0:T(8,128)(2,1)S(1)} %copy-done.2, bf16[2,128,128]{2,1,0:T(8,128)(2,1)S(1)} %copy-done.3, f32[2,128]{1,0:T(2,128)S(1)} %copy-done.6, ...), custom_call_target="tpu_custom_call" | custom-call | tf_op jit(solution)/shard_map/triangle/pallas_call | solution.py:260
  67.5 0.8 %copy.9 = bf16[64,32,128]{2,1,0:T(8,128)(2,1)} copy(bf16[64,32,128]{2,1,0:T(8,128)(2,1)S(1)} %triangle.1) | data formatting | bytes 1048576
Async XLA Ops:
  0.0 1.0 %copy-start = (bf16[64,32,128]{2,1,0:T(8,128)(2,1)S(1)}, bf16[64,32,128]{2,1,0:T(8,128)(2,1)}, u32[]{:S(2)}) copy-start(bf16[64,32,128]{2,1,0:T(8,128)(2,1)} %pair_hbm.1) | copy-start | bytes 1572868
  1.0 0.9 %copy-start.1 = (bf16[2,128,256]{2,1,0:T(8,128)(2,1)S(1)}, bf16[2,128,256]{2,1,0:T(8,128)(2,1)}, u32[]{:S(2)}) copy-start(bf16[2,128,256]{2,1,0:T(8,128)(2,1)} %w_left_hbm.1) | copy-start | bytes 393220
  1.9 0.9 %copy-start.2 = (bf16[2,128,256]{2,1,0:T(8,128)(2,1)S(1)}, bf16[2,128,256]{2,1,0:T(8,128)(2,1)}, u32[]{:S(2)}) copy-start(bf16[2,128,256]{2,1,0:T(8,128)(2,1)} %w_right_hbm.1) | copy-start | bytes 393220
  2.9 0.8 %copy-start.3 = (bf16[2,128,128]{2,1,0:T(8,128)(2,1)S(1)}, bf16[2,128,128]{2,1,0:T(8,128)(2,1)}, u32[]{:S(2)}) copy-start(bf16[2,128,128]{2,1,0:T(8,128)(2,1)} %w_gate_hbm.1) | copy-start | bytes 196612
  3.7 0.8 %copy-start.4 = (bf16[2,128,128]{2,1,0:T(8,128)(2,1)S(1)}, bf16[2,128,128]{2,1,0:T(8,128)(2,1)}, u32[]{:S(2)}) copy-start(bf16[2,128,128]{2,1,0:T(8,128)(2,1)} %w_out_hbm.1) | copy-start | bytes 196612
  4.5 0.7 copy-start.5
  5.2 0.7 copy-start.6

commit v3 on v2

v3 whole, which is shorter than its diff:
```python
import itertools

import jax
import jax.numpy as jnp
from jax import lax
from jax.experimental import pallas as pl
from jax.experimental.pallas import tpu as pltpu
from jax.sharding import PartitionSpec as P


MESH = pl.DeviceIdType.MESH
F32, BF16 = jnp.float32, jnp.bfloat16
EPS = 1e-05
GROUPS = ((1, 3), (2, 0))


def hops(steps):
    return sum(min(d, 4 - d) for d in steps[:3])


ALL = sorted(itertools.product(range(4), range(4), range(4), range(2)), key=lambda d: (-hops(d), -d[3]))


def norm_rows(values, gain):
    mean = jnp.mean(values, axis=0, keepdims=True)
    centred = values - mean
    spread = jnp.mean(centred * centred, axis=0, keepdims=True)
    return centred * lax.rsqrt(spread + EPS) * gain


def turned(matrix):
    return jnp.transpose(matrix.astype(F32))


def swap_halves(first, second):
    low = jnp.concatenate([first[:, :64], second[:, :64]], axis=1)
    high = jnp.concatenate([first[:, 64:], second[:, 64:]], axis=1)
    return low, high


def at(index, unit, count=1):
    return pl.ds(pl.multiple_of(index * unit, unit), unit * count)


def kernel(
    pair_hbm, ln_in_hbm, w_left_hbm, w_right_hbm, w_gate_hbm, ln_out_hbm, w_out_hbm, out_ref,
    pair_ref, ln_in_ref, w_left_ref, w_right_ref, w_gate_ref, ln_out_ref, w_out_ref,
    flat, tile, normed, gate, spread_buf, w_proj, w_turn, right_t, left_low, left_high,
    send_l, send_r, send_e, recv_l, recv_r, recv_e,
    load_sem, send_sem, first_sem, second_sem, edge_sem,
):
    row, col = lax.axis_index("row"), lax.axis_index("col")
    x, y, z, core = row // 2, ((col // 2) % 2) * 2 + row % 2, col // 4, col % 2
    xs = [(x + d) % 4 for d in range(4)]
    ys = [(y + d) % 4 for d in range(4)]
    zs = [(z + d) % 4 for d in range(4)]
    cores = [core, 1 - core]
    y_low = [v % 2 for v in ys]
    y_high = [(v // 2) * 2 for v in ys]

    def device(steps):
        dx, dy, dz, dc = steps
        return xs[dx] * 2 + y_low[dy], zs[dz] * 4 + y_high[dy] + cores[dc]

    def channel(u, steps):
        dx, dy, dz, dc = steps
        plane, third = ((xs[dx], zs[dz]), (zs[dz], xs[dx]))[u]
        return (plane * 2 + cores[dc]) * 16 + ys[dy] * 4 + third

    loads = []
    pairs = (
        (pair_hbm, pair_ref), (ln_in_hbm, ln_in_ref), (w_right_hbm, w_right_ref), (w_left_hbm, w_left_ref),
        (w_gate_hbm, w_gate_ref), (ln_out_hbm, ln_out_ref), (w_out_hbm, w_out_ref),
    )
    for n, (src, dst) in enumerate(pairs):
        loads.append(pltpu.make_async_copy(src, dst, load_sem.at[n]))
        loads[-1].start()

    barrier = pltpu.get_barrier_semaphore()
    for steps in ALL:
        if any(steps):
            pl.semaphore_signal(barrier, inc=1, device_id=device(steps), device_id_type=MESH)

    def prepare(u, side):
        both = turned((w_left_ref, w_right_ref)[side][u]).astype(BF16)
        for j in range(4):
            w_proj[u, side, j, 0:32] = both[32 * j : 32 * j + 32]
            w_proj[u, side, j, 32:64] = both[128 + 32 * j : 160 + 32 * j]

    def gain_of(ref, u):
        return jnp.transpose(jnp.broadcast_to(ref[u : u + 1, :], (128, 128)))

    loads[0].wait()
    loads[1].wait()
    flat[...] = pair_ref[...].reshape(2048, 128).astype(F32)
    gain_in = gain_of(ln_in_ref, 0)
    for s in range(16):
        block = jnp.concatenate(
            [flat[pl.ds(s, 64, stride=32), :], flat[pl.ds(16 + s, 64, stride=32), :]], axis=0
        )
        block = jnp.transpose(block)
        tile[:, s * 128 : s * 128 + 128] = block.astype(BF16)
        normed[:, s * 128 : s * 128 + 128] = norm_rows(block, gain_in).astype(BF16)

    def send_to(src, dst, out_sem, in_sem, steps):
        if any(steps):
            pltpu.make_async_remote_copy(
                src_ref=src, dst_ref=dst, send_sem=out_sem, recv_sem=in_sem,
                device_id=device(steps), device_id_type=MESH,
            ).start()
        else:
            pltpu.make_async_copy(src, dst, in_sem).start()

    def project(u, side, plane, send):
        for part in range(4):
            p = jnp.dot(
                w_proj[u, side, plane], normed[:, part * 512 : part * 512 + 512], preferred_element_type=F32
            )
            value = jax.nn.sigmoid(p[:32]) * p[32:]
            for s in range(4):
                spread_buf[pl.ds(part * 4 + s, 32, stride=16), :] = value[:, s * 128 : s * 128 + 128]
        send[u, at(plane, 512), :] = spread_buf[0:512, :].astype(BF16)

    loads[2].wait()
    prepare(0, 1)

    def project_all(j, carry):
        project(0, 1, j, send_r)
        return carry

    lax.fori_loop(0, 4, project_all, 0)
    pl.semaphore_wait(barrier, 127)

    for u in range(2):
        axis = (0, 2)[u]
        planes = (xs, zs)[u]
        slot = (row * 16 + col, z * 32 + row * 4 + col % 4)[u]
        side, send, recv = ((1, send_r, recv_r), (0, send_l, recv_l))[u]

        def send_first(steps):
            send_to(
                send.at[u, at(channel(u, steps), 16), :], recv.at[u, at(slot, 16), :],
                send_sem.at[u, 0], first_sem.at[u, steps[axis]], steps,
            )

        if u == 0:
            for steps in ALL:
                send_first(steps)
        else:
            for d in GROUPS[0] + GROUPS[1]:
                project(u, side, planes[d], send)
                for steps in ALL:
                    if steps[axis] == d:
                        send_first(steps)

        side, send, recv = ((0, send_l, recv_l), (1, send_r, recv_r))[u]
        if u == 0:
            loads[3].wait()
            prepare(0, 0)
        for n, group in enumerate(GROUPS):
            for d in group:
                project(u, side, planes[d], send)
            for steps in ALL:
                if steps[axis] in group:
                    send_to(
                        send.at[u, at(channel(u, steps), 16), :], recv.at[u, at(slot, 16), :],
                        send_sem.at[u, 1], second_sem.at[u, n], steps,
                    )

        if u == 0:
            prepare(1, 0)
            prepare(1, 1)
            for n in (4, 5, 6):
                loads[n].wait()
            for v in range(2):
                w_turn[v, 0] = turned(w_gate_ref[v]).astype(BF16)
                w_turn[v, 1] = turned(w_out_ref[v]).astype(BF16)
        gate[...] = jax.nn.sigmoid(jnp.dot(w_turn[u, 0], normed[...], preferred_element_type=F32))

        def arrived(recv, sem, count):
            some = recv.at[u, pl.ds(0, 16 * count), :]
            pltpu.make_async_copy(some, some, sem).wait()

        for d in GROUPS[0] + GROUPS[1]:
            g = planes[-d % 4]
            if u == 0:
                arrived(recv_r, first_sem.at[u, d], 32)
                for half in range(2):
                    r = 2 * g + half
                    right_t[at(r, 128), :] = turned(recv_r[u, at(r, 256), :]).astype(BF16)
            else:
                arrived(recv_l, first_sem.at[u, d], 32)
                for r in range(8):
                    here = recv_l[u, at(32 * g + 4 * r, 16, 4), :]
                    none = jnp.zeros((64, 64), BF16)
                    lanes = slice(r * 128, r * 128 + 128)
                    for half in range(2):
                        part = here[:, half * 64 : half * 64 + 64]
                        low = jnp.concatenate([part, none], axis=1)
                        high = jnp.concatenate([none, part], axis=1)
                        for c in range(4):
                            rows = at(8 * g + 2 * c + half, 16)
                            left_low[rows, lanes] = low[c * 16 : c * 16 + 16]
                            left_high[rows, lanes] = high[c * 16 : c * 16 + 16]

        for n, group in enumerate(GROUPS):
            sources = [planes[-d % 4] for d in group]
            if u == 0:
                arrived(recv_l, second_sem.at[u, n], 64)
                left = jnp.concatenate(
                    [recv_l[u, at(2 * g + half, 256), :] for g in sources for half in range(2)], axis=1
                )
                is_low = lax.broadcasted_iota(jnp.int32, (16, 128), 1) < 64
                for r in range(8):
                    both = jnp.dot(
                        right_t[r * 128 : r * 128 + 128, :], left, preferred_element_type=F32
                    )
                    for k in range(4):
                        block = both[:, k * 128 : k * 128 + 128]
                        for c in range(2):
                            top = block[c * 32 : c * 32 + 32]
                            bottom = block[64 + c * 32 : 96 + c * 32]
                            edges = jnp.where(is_low, top[:16], bottom[16:]) + pltpu.roll(
                                jnp.where(is_low, top[16:], bottom[:16]), 64, 1
                            )
                            to = (n * 64 + k * 16 + 2 * r + c) * 16
                            send_e[u, to : to + 16, :] = edges.astype(BF16)
            else:
                arrived(recv_r, second_sem.at[u, n], 64)
                right = jnp.concatenate(
                    [
                        jnp.concatenate([recv_r[u, at(32 * g + 4 * r, 16, 4), :] for r in range(8)], axis=1)
                        for g in sources
                    ],
                    axis=0,
                )
                contract = (((1,), (1,)), ((), ()))
                first = lax.dot_general(right, left_low[...], contract, preferred_element_type=F32)
                second = lax.dot_general(right, left_high[...], contract, preferred_element_type=F32)
                first, second = first.astype(BF16), second.astype(BF16)
                for k in range(8):
                    for m in range(4):
                        part = (slice(k * 16, k * 16 + 16), slice(m * 128, m * 128 + 128))
                        low, high = swap_halves(first[part], second[part])
                        to = (n * 64 + k * 8 + 2 * m) * 16
                        send_e[u, to : to + 16, :] = low
                        send_e[u, to + 16 : to + 32, :] = high
            for steps in ALL:
                back = -steps[axis] % 4
                if back in group:
                    pr, pc = device(steps)
                    there = (pr % 2 * 16 + pc, pc % 4 * 8 + pr)[u] + (n * 2 + group.index(back)) * 32
                    send_to(
                        send_e.at[u, at(there, 16), :], recv_e.at[u, at(channel(u, (0, 0, 0, 0)), 16), :],
                        send_sem.at[u, 2], edge_sem.at[u], steps,
                    )

        gain_out = gain_of(ln_out_ref, u)
        gain_next = gain_of(ln_in_ref, 1)
        arrived(recv_e, edge_sem.at[u], 128)
        spread_buf[...] = recv_e[u].astype(F32)
        for s in range(16):
            lanes = slice(s * 128, s * 128 + 128)
            scaled = norm_rows(spread_buf[pl.ds(s, 128, stride=16), :], gain_out).astype(BF16)
            update = jnp.dot(w_turn[u, 1], scaled, preferred_element_type=F32)
            updated = tile[:, lanes].astype(F32) + gate[:, lanes] * update
            if u == 0:
                rounded = updated.astype(BF16)
                tile[:, lanes] = rounded
                normed[:, lanes] = norm_rows(rounded.astype(F32), gain_next).astype(BF16)
            else:
                block = jnp.transpose(updated)
                flat[pl.ds(s, 64, stride=32), :] = block[:64]
                flat[pl.ds(16 + s, 64, stride=32), :] = block[64:]
    out_ref[...] = flat[...].astype(BF16).reshape(64, 32, 128)

    for u in range(2):
        for n in range(3):
            sent = send_e.at[u, pl.ds(0, 127 * 16), :]
            pltpu.make_async_copy(sent, sent, send_sem.at[u, n]).wait()


def local(*args):
    tokens = pltpu.VMEM((2, 2048, 128), BF16)
    return pl.pallas_call(
        kernel,
        out_shape=jax.ShapeDtypeStruct((64, 32, 128), BF16),
        in_specs=[pl.BlockSpec(memory_space=pl.ANY)] * 7,
        out_specs=pl.BlockSpec(memory_space=pltpu.VMEM),
        scratch_shapes=[pltpu.VMEM(arg.shape, arg.dtype) for arg in args]
        + [
            pltpu.VMEM((2048, 128), F32),
            pltpu.VMEM((128, 2048), BF16),
            pltpu.VMEM((128, 2048), BF16),
            pltpu.VMEM((128, 2048), F32),
            pltpu.VMEM((2048, 128), F32),
            pltpu.VMEM((2, 2, 4, 64, 128), BF16),
            pltpu.VMEM((2, 2, 128, 128), BF16),
            pltpu.VMEM((1024, 256), BF16),
            pltpu.VMEM((512, 1024), BF16),
            pltpu.VMEM((512, 1024), BF16),
            tokens, tokens, tokens, tokens, tokens, tokens,
            pltpu.SemaphoreType.DMA((7,)),
            pltpu.SemaphoreType.DMA((2, 3)),
            pltpu.SemaphoreType.DMA((2, 4)),
            pltpu.SemaphoreType.DMA((2, 2)),
            pltpu.SemaphoreType.DMA((2,)),
        ],
        compiler_params=pltpu.CompilerParams(
            collective_id=0, has_side_effects=True, vmem_limit_bytes=48 << 20
        ),
        name="triangle",
    )(*[pltpu.with_memory_space_constraint(arg, pltpu.HBM) for arg in args])


def solution(mesh):
    return jax.shard_map(
        local,
        mesh=mesh,
        in_specs=(P("row", "col", None), P(), P(), P(), P(), P(), P()),
        out_specs=P("row", "col", None),
        check_vma=False,
    )
```

time: 68.6 us -> 60.4 us (0.88)
  local copies, waits for them, and re-layouts: 6.68 us -> 0.8 us
  Pallas kernels: 61.6 us -> 59.5 us
    unnamed x15 -> x1, local copies, waits for them, and re-layouts: 6.68 us -> 0.8 us
    pallas_call x1, Pallas kernels: 61.6 us -> 59.5 us  [local(): pl.pallas_call(kernel, out_shape=jax.ShapeDtypeStruct((64, 32, 128), BF16...]
where the time goes in v3:
time: 60.4 us; the launch traced here: 60.3 us
  Pallas kernels  59.5 us (99%)
  local copies, waits for them, and re-layouts  0.8 us (1%)
    pallas_call x1, Pallas kernels, local(): pl.pallas_call(kernel, out_shape=jax.ShapeDtypeStruct((64, 32, 128), BF16...  59.5 us

profile of v3, /device:TPU:1, one launch (start us, length us, event | category | flops | bytes accessed | tf_op | source)
XLA Modules:
  0.0 60.3 jit_solution(7019531743696622755)
XLA Ops:
  0.0 59.5 %triangle.1 = bf16[64,32,128]{2,1,0:T(8,128)(2,1)S(1)} custom-call(bf16[64,32,128]{2,1,0:T(8,128)(2,1)} %pair_hbm.1, f32[2,128]{1,0:T(2,128)} %ln_in_hbm.1, bf16[2,128,256]{2,1,0:T(8,128)(2,1)} %w_left_hbm.1, bf16[2,128,256]{2,1,0:T(8,128)(2,1)} %w_right_hbm.1, bf16[2,128,128]{2,1,0:T(8,128)(2,1)} %w_gate_hbm.1, f32[2,128]{1,0:T(2,128)} %ln_out_hbm.1, ...), custom_call_target="tpu_custom_call" | custom-call | tf_op jit(solution)/shard_map/triangle/pallas_call | solution.py:285
  59.5 0.8 %copy.9 = bf16[64,32,128]{2,1,0:T(8,128)(2,1)} copy(bf16[64,32,128]{2,1,0:T(8,128)(2,1)S(1)} %triangle.1) | data formatting | bytes 1048576

commit v4 on v3

--- a/solution.py
+++ b/solution.py
@@ -12,6 +12,7 @@
 F32, BF16 = jnp.float32, jnp.bfloat16
 EPS = 1e-05
 GROUPS = ((1, 3), (2, 0))
+OTHERS = ((1, 1), (1, 0), (0, 1), (0, 0))
 
 
 def hops(steps):
@@ -64,8 +65,12 @@
 
     def channel(u, steps):
         dx, dy, dz, dc = steps
-        plane, third = ((xs[dx], zs[dz]), (zs[dz], xs[dx]))[u]
-        return (plane * 2 + cores[dc]) * 16 + ys[dy] * 4 + third
+        if u == 0:
+            return (xs[dx] * 2 + cores[dc]) * 16 + ys[dy] * 4 + zs[dz]
+        return (cores[dc] * 2 + xs[dx] % 2) * 32 + (xs[dx] // 2) * 16 + ys[dy] * 4 + zs[dz]
+
+    def group_of(u, steps):
+        return 1 - steps[0] % 2 if u == 0 else 1 - steps[3]
 
     loads = []
     pairs = (
@@ -92,11 +97,12 @@
 
     loads[0].wait()
     loads[1].wait()
-    flat[...] = pair_ref[...].reshape(2048, 128).astype(F32)
+    for ii in range(64):
+        flat[ii * 40 : ii * 40 + 32, :] = pair_ref[ii].astype(F32)
     gain_in = gain_of(ln_in_ref, 0)
     for s in range(16):
         block = jnp.concatenate(
-            [flat[pl.ds(s, 64, stride=32), :], flat[pl.ds(16 + s, 64, stride=32), :]], axis=0
+            [flat[pl.ds(s, 64, stride=40), :], flat[pl.ds(16 + s, 64, stride=40), :]], axis=0
         )
         block = jnp.transpose(block)
         tile[:, s * 128 : s * 128 + 128] = block.astype(BF16)
@@ -111,15 +117,16 @@
         else:
             pltpu.make_async_copy(src, dst, in_sem).start()
 
-    def project(u, side, plane, send):
+    def project(u, side, chunk, send):
         for part in range(4):
             p = jnp.dot(
-                w_proj[u, side, plane], normed[:, part * 512 : part * 512 + 512], preferred_element_type=F32
+                w_proj[u, side, chunk], normed[:, part * 512 : part * 512 + 512], preferred_element_type=F32
             )
             value = jax.nn.sigmoid(p[:32]) * p[32:]
             for s in range(4):
-                spread_buf[pl.ds(part * 4 + s, 32, stride=16), :] = value[:, s * 128 : s * 128 + 128]
-        send[u, at(plane, 512), :] = spread_buf[0:512, :].astype(BF16)
+                spread_buf[pl.ds(part * 4 + s, 32, stride=24), :] = value[:, s * 128 : s * 128 + 128]
+        for h in range(32):
+            send[u, at(chunk * 32 + h, 16), :] = spread_buf[h * 24 : h * 24 + 16, :].astype(BF16)
 
     loads[2].wait()
     prepare(0, 1)
@@ -132,25 +139,23 @@
     pl.semaphore_wait(barrier, 127)
 
     for u in range(2):
-        axis = (0, 2)[u]
-        planes = (xs, zs)[u]
-        slot = (row * 16 + col, z * 32 + row * 4 + col % 4)[u]
+        slot = (row * 16 + col, core * 64 + row * 8 + col // 2)[u]
         side, send, recv = ((1, send_r, recv_r), (0, send_l, recv_l))[u]
 
         def send_first(steps):
             send_to(
                 send.at[u, at(channel(u, steps), 16), :], recv.at[u, at(slot, 16), :],
-                send_sem.at[u, 0], first_sem.at[u, steps[axis]], steps,
+                send_sem.at[u, 0], first_sem.at[u, steps[3 * u]], steps,
             )
 
         if u == 0:
             for steps in ALL:
                 send_first(steps)
         else:
-            for d in GROUPS[0] + GROUPS[1]:
-                project(u, side, planes[d], send)
+            for dc, odd in OTHERS:
+                project(u, side, cores[dc] * 2 + xs[odd] % 2, send)
                 for steps in ALL:
-                    if steps[axis] == d:
+                    if (steps[3], steps[0] % 2) == (dc, odd):
                         send_first(steps)
 
         side, send, recv = ((0, send_l, recv_l), (1, send_r, recv_r))[u]
@@ -158,10 +163,10 @@
             loads[3].wait()
             prepare(0, 0)
         for n, group in enumerate(GROUPS):
-            for d in group:
-                project(u, side, planes[d], send)
+            for k in range(2):
+                project(u, side, xs[group[k]] if u == 0 else cores[1 - n] * 2 + k, send)
             for steps in ALL:
-                if steps[axis] in group:
+                if group_of(u, steps) == n:
                     send_to(
                         send.at[u, at(channel(u, steps), 16), :], recv.at[u, at(slot, 16), :],
                         send_sem.at[u, 1], second_sem.at[u, n], steps,
@@ -181,31 +186,32 @@
             some = recv.at[u, pl.ds(0, 16 * count), :]
             pltpu.make_async_copy(some, some, sem).wait()
 
-        for d in GROUPS[0] + GROUPS[1]:
-            g = planes[-d % 4]
+        for d in (1, 3, 2, 0) if u == 0 else (1, 0):
             if u == 0:
+                g = xs[-d % 4]
                 arrived(recv_r, first_sem.at[u, d], 32)
                 for half in range(2):
                     r = 2 * g + half
                     right_t[at(r, 128), :] = turned(recv_r[u, at(r, 256), :]).astype(BF16)
             else:
-                arrived(recv_l, first_sem.at[u, d], 32)
+                g = cores[d]
+                arrived(recv_l, first_sem.at[u, d], 64)
                 for r in range(8):
-                    here = recv_l[u, at(32 * g + 4 * r, 16, 4), :]
-                    none = jnp.zeros((64, 64), BF16)
+                    here = recv_l[u, at(64 * g + 8 * r, 16, 8), :]
+                    none = jnp.zeros((128, 64), BF16)
                     lanes = slice(r * 128, r * 128 + 128)
                     for half in range(2):
                         part = here[:, half * 64 : half * 64 + 64]
                         low = jnp.concatenate([part, none], axis=1)
                         high = jnp.concatenate([none, part], axis=1)
-                        for c in range(4):
-                            rows = at(8 * g + 2 * c + half, 16)
+                        for c in range(8):
+                            rows = at(4 * c + 2 * g + half, 16)
                             left_low[rows, lanes] = low[c * 16 : c * 16 + 16]
                             left_high[rows, lanes] = high[c * 16 : c * 16 + 16]
 
         for n, group in enumerate(GROUPS):
-            sources = [planes[-d % 4] for d in group]
             if u == 0:
+                sources = [xs[-d % 4] for d in group]
                 arrived(recv_l, second_sem.at[u, n], 64)
                 left = jnp.concatenate(
                     [recv_l[u, at(2 * g + half, 256), :] for g in sources for half in range(2)], axis=1
@@ -227,13 +233,8 @@
                             send_e[u, to : to + 16, :] = edges.astype(BF16)
             else:
                 arrived(recv_r, second_sem.at[u, n], 64)
-                right = jnp.concatenate(
-                    [
-                        jnp.concatenate([recv_r[u, at(32 * g + 4 * r, 16, 4), :] for r in range(8)], axis=1)
-                        for g in sources
-                    ],
-                    axis=0,
-                )
+                g = cores[1 - n]
+                right = jnp.concatenate([recv_r[u, at(64 * g + 8 * r, 16, 8), :] for r in range(8)], axis=1)
                 contract = (((1,), (1,)), ((), ()))
                 first = lax.dot_general(right, left_low[...], contract, preferred_element_type=F32)
                 second = lax.dot_general(right, left_high[...], contract, preferred_element_type=F32)
@@ -246,22 +247,28 @@
                         send_e[u, to : to + 16, :] = low
                         send_e[u, to + 16 : to + 32, :] = high
             for steps in ALL:
-                back = -steps[axis] % 4
-                if back in group:
+                if group_of(u, steps) == n:
                     pr, pc = device(steps)
-                    there = (pr % 2 * 16 + pc, pc % 4 * 8 + pr)[u] + (n * 2 + group.index(back)) * 32
+                    if u == 0:
+                        there = (n * 2 + group.index(-steps[0] % 4)) * 32 + pr % 2 * 16 + pc
+                    else:
+                        there = n * 64 + (pc // 2) * 8 + pr
                     send_to(
                         send_e.at[u, at(there, 16), :], recv_e.at[u, at(channel(u, (0, 0, 0, 0)), 16), :],
-                        send_sem.at[u, 2], edge_sem.at[u], steps,
+                        send_sem.at[u, 2], edge_sem.at[u, n], steps,
                     )
 
         gain_out = gain_of(ln_out_ref, u)
         gain_next = gain_of(ln_in_ref, 1)
-        arrived(recv_e, edge_sem.at[u], 128)
-        spread_buf[...] = recv_e[u].astype(F32)
+        for n, group in enumerate(GROUPS):
+            arrived(recv_e, edge_sem.at[u, n], 64)
+            for k in range(2):
+                base = xs[group[k]] * 32 if u == 0 else cores[1 - n] * 64 + k * 32
+                for h in range(32):
+                    spread_buf[at(base * 3 + h * 3, 8, 2), :] = recv_e[u, at(base + h, 16), :].astype(F32)
         for s in range(16):
             lanes = slice(s * 128, s * 128 + 128)
-            scaled = norm_rows(spread_buf[pl.ds(s, 128, stride=16), :], gain_out).astype(BF16)
+            scaled = norm_rows(spread_buf[pl.ds(s, 128, stride=24), :], gain_out).astype(BF16)
             update = jnp.dot(w_turn[u, 1], scaled, preferred_element_type=F32)
             updated = tile[:, lanes].astype(F32) + gate[:, lanes] * update
             if u == 0:
@@ -270,9 +277,10 @@
                 normed[:, lanes] = norm_rows(rounded.astype(F32), gain_next).astype(BF16)
             else:
                 block = jnp.transpose(updated)
-                flat[pl.ds(s, 64, stride=32), :] = block[:64]
-                flat[pl.ds(16 + s, 64, stride=32), :] = block[64:]
-    out_ref[...] = flat[...].astype(BF16).reshape(64, 32, 128)
+                flat[pl.ds(s, 64, stride=40), :] = block[:64]
+                flat[pl.ds(16 + s, 64, stride=40), :] = block[64:]
+    for ii in range(64):
+        out_ref[ii] = flat[ii * 40 : ii * 40 + 32, :].astype(BF16)
 
     for u in range(2):
         for n in range(3):
@@ -289,11 +297,11 @@
         out_specs=pl.BlockSpec(memory_space=pltpu.VMEM),
         scratch_shapes=[pltpu.VMEM(arg.shape, arg.dtype) for arg in args]
         + [
-            pltpu.VMEM((2048, 128), F32),
+            pltpu.VMEM((64 * 40, 128), F32),
             pltpu.VMEM((128, 2048), BF16),
             pltpu.VMEM((128, 2048), BF16),
             pltpu.VMEM((128, 2048), F32),
-            pltpu.VMEM((2048, 128), F32),
+            pltpu.VMEM((128 * 24, 128), F32),
             pltpu.VMEM((2, 2, 4, 64, 128), BF16),
             pltpu.VMEM((2, 2, 128, 128), BF16),
             pltpu.VMEM((1024, 256), BF16),
@@ -304,7 +312,7 @@
             pltpu.SemaphoreType.DMA((2, 3)),
             pltpu.SemaphoreType.DMA((2, 4)),
             pltpu.SemaphoreType.DMA((2, 2)),
-            pltpu.SemaphoreType.DMA((2,)),
+            pltpu.SemaphoreType.DMA((2, 2)),
         ],
         compiler_params=pltpu.CompilerParams(
             collective_id=0, has_side_effects=True, vmem_limit_bytes=48 << 20

time: 60.4 us -> 59.3 us (0.982)
  Pallas kernels: 59.5 us -> 58.4 us
    pallas_call x1, Pallas kernels: 59.5 us -> 58.4 us  [local(): pl.pallas_call(kernel, out_shape=jax.ShapeDtypeStruct((64, 32, 128), BF16...]
where the time goes in v4:
time: 59.3 us; the launch traced here: 59.2 us
  Pallas kernels  58.4 us (98%)
  local copies, waits for them, and re-layouts  0.8 us (1%)
    pallas_call x1, Pallas kernels, local(): pl.pallas_call(kernel, out_shape=jax.ShapeDtypeStruct((64, 32, 128), BF16...  58.4 us

profile of v4, /device:TPU:1, one launch (start us, length us, event | category | flops | bytes accessed | tf_op | source)
XLA Modules:
  0.0 59.2 jit_solution(11695015896159790804)
XLA Ops:
  0.0 58.4 %triangle.1 = bf16[64,32,128]{2,1,0:T(8,128)(2,1)S(1)} custom-call(bf16[64,32,128]{2,1,0:T(8,128)(2,1)} %pair_hbm.1, f32[2,128]{1,0:T(2,128)} %ln_in_hbm.1, bf16[2,128,256]{2,1,0:T(8,128)(2,1)} %w_left_hbm.1, bf16[2,128,256]{2,1,0:T(8,128)(2,1)} %w_right_hbm.1, bf16[2,128,128]{2,1,0:T(8,128)(2,1)} %w_gate_hbm.1, f32[2,128]{1,0:T(2,128)} %ln_out_hbm.1, ...), custom_call_target="tpu_custom_call" | custom-call | tf_op jit(solution)/shard_map/triangle/pallas_call | solution.py:293
  58.4 0.8 %copy.9 = bf16[64,32,128]{2,1,0:T(8,128)(2,1)} copy(bf16[64,32,128]{2,1,0:T(8,128)(2,1)S(1)} %triangle.1) | data formatting | bytes 1048576

commit v5 on v4

--- a/solution.py
+++ b/solution.py
@@ -46,7 +46,7 @@
 def kernel(
     pair_hbm, ln_in_hbm, w_left_hbm, w_right_hbm, w_gate_hbm, ln_out_hbm, w_out_hbm, out_ref,
     pair_ref, ln_in_ref, w_left_ref, w_right_ref, w_gate_ref, ln_out_ref, w_out_ref,
-    flat, tile, normed, gate, spread_buf, w_proj, w_turn, right_t, left_low, left_high,
+    flat, tile, normed, gate, spread_buf, w_proj, w_turn, right_t, left_rows,
     send_l, send_r, send_e, recv_l, recv_r, recv_e,
     load_sem, send_sem, first_sem, second_sem, edge_sem,
 ):
@@ -186,59 +186,58 @@
             some = recv.at[u, pl.ds(0, 16 * count), :]
             pltpu.make_async_copy(some, some, sem).wait()
 
+        def side_by_side(recv, first):
+            return swap_halves(recv[u, at(first, 16, 8), :], recv[u, at(first + 8, 16, 8), :])
+
         for d in (1, 3, 2, 0) if u == 0 else (1, 0):
             if u == 0:
                 g = xs[-d % 4]
                 arrived(recv_r, first_sem.at[u, d], 32)
-                for half in range(2):
-                    r = 2 * g + half
-                    right_t[at(r, 128), :] = turned(recv_r[u, at(r, 256), :]).astype(BF16)
+                low, high = swap_halves(recv_r[u, at(2 * g, 256), :], recv_r[u, at(2 * g + 1, 256), :])
+                right_t[at(g, 128), 0:256] = turned(low).astype(BF16)
+                right_t[at(g, 128), 256:512] = turned(high).astype(BF16)
             else:
                 g = cores[d]
                 arrived(recv_l, first_sem.at[u, d], 64)
-                for r in range(8):
-                    here = recv_l[u, at(64 * g + 8 * r, 16, 8), :]
-                    none = jnp.zeros((128, 64), BF16)
-                    lanes = slice(r * 128, r * 128 + 128)
+                for m in range(4):
+                    halves = side_by_side(recv_l, 64 * g + 16 * m)
                     for half in range(2):
-                        part = here[:, half * 64 : half * 64 + 64]
-                        low = jnp.concatenate([part, none], axis=1)
-                        high = jnp.concatenate([none, part], axis=1)
                         for c in range(8):
-                            rows = at(4 * c + 2 * g + half, 16)
-                            left_low[rows, lanes] = low[c * 16 : c * 16 + 16]
-                            left_high[rows, lanes] = high[c * 16 : c * 16 + 16]
+                            left_rows[at(4 * c + 2 * g + half, 16), m * 128 : m * 128 + 128] = halves[half][
+                                c * 16 : c * 16 + 16
+                            ]
 
         for n, group in enumerate(GROUPS):
             if u == 0:
                 sources = [xs[-d % 4] for d in group]
                 arrived(recv_l, second_sem.at[u, n], 64)
+                pairs = [
+                    swap_halves(recv_l[u, at(2 * g, 256), :], recv_l[u, at(2 * g + 1, 256), :]) for g in sources
+                ]
                 left = jnp.concatenate(
-                    [recv_l[u, at(2 * g + half, 256), :] for g in sources for half in range(2)], axis=1
+                    [jnp.concatenate([pair[half] for pair in pairs], axis=1) for half in range(2)], axis=0
                 )
-                is_low = lax.broadcasted_iota(jnp.int32, (16, 128), 1) < 64
-                for r in range(8):
-                    both = jnp.dot(
-                        right_t[r * 128 : r * 128 + 128, :], left, preferred_element_type=F32
-                    )
-                    for k in range(4):
-                        block = both[:, k * 128 : k * 128 + 128]
-                        for c in range(2):
-                            top = block[c * 32 : c * 32 + 32]
-                            bottom = block[64 + c * 32 : 96 + c * 32]
-                            edges = jnp.where(is_low, top[:16], bottom[16:]) + pltpu.roll(
-                                jnp.where(is_low, top[16:], bottom[:16]), 64, 1
-                            )
-                            to = (n * 64 + k * 16 + 2 * r + c) * 16
-                            send_e[u, to : to + 16, :] = edges.astype(BF16)
+                edges = jnp.dot(right_t[...], left, preferred_element_type=F32).astype(BF16)
+                for c in range(16):
+                    for k in range(2):
+                        lanes = slice(k * 128, k * 128 + 128)
+                        low, high = swap_halves(
+                            edges[c * 32 : c * 32 + 16, lanes], edges[c * 32 + 16 : c * 32 + 32, lanes]
+                        )
+                        to = (n * 64 + k * 32 + c) * 16
+                        send_e[u, to : to + 16, :] = low
+                        send_e[u, to + 256 : to + 272, :] = high
             else:
                 arrived(recv_r, second_sem.at[u, n], 64)
                 g = cores[1 - n]
-                right = jnp.concatenate([recv_r[u, at(64 * g + 8 * r, 16, 8), :] for r in range(8)], axis=1)
-                contract = (((1,), (1,)), ((), ()))
-                first = lax.dot_general(right, left_low[...], contract, preferred_element_type=F32)
-                second = lax.dot_general(right, left_high[...], contract, preferred_element_type=F32)
-                first, second = first.astype(BF16), second.astype(BF16)
+                pairs = [side_by_side(recv_r, 64 * g + 16 * m) for m in range(4)]
+                right = jnp.concatenate(
+                    [jnp.concatenate([pair[half] for pair in pairs], axis=1) for half in range(2)], axis=0
+                )
+                edges = lax.dot_general(
+                    right, left_rows[...], (((1,), (1,)), ((), ())), preferred_element_type=F32
+                ).astype(BF16)
+                first, second = edges[:128], edges[128:]
                 for k in range(8):
                     for m in range(4):
                         part = (slice(k * 16, k * 16 + 16), slice(m * 128, m * 128 + 128))
@@ -304,9 +303,8 @@
             pltpu.VMEM((128 * 24, 128), F32),
             pltpu.VMEM((2, 2, 4, 64, 128), BF16),
             pltpu.VMEM((2, 2, 128, 128), BF16),
-            pltpu.VMEM((1024, 256), BF16),
-            pltpu.VMEM((512, 1024), BF16),
-            pltpu.VMEM((512, 1024), BF16),
+            pltpu.VMEM((512, 512), BF16),
+            pltpu.VMEM((512, 512), BF16),
             tokens, tokens, tokens, tokens, tokens, tokens,
             pltpu.SemaphoreType.DMA((7,)),
             pltpu.SemaphoreType.DMA((2, 3)),

time: 59.3 us -> 58.5 us (0.987)
  Pallas kernels: 58.4 us -> 57.4 us
    pallas_call x1, Pallas kernels: 58.4 us -> 57.4 us  [local(): pl.pallas_call(kernel, out_shape=jax.ShapeDtypeStruct((64, 32, 128), BF16...]
where the time goes in v5:
time: 58.5 us; the launch traced here: 58.2 us
  Pallas kernels  57.4 us (98%)
  local copies, waits for them, and re-layouts  0.8 us (1%)
    pallas_call x1, Pallas kernels, local(): pl.pallas_call(kernel, out_shape=jax.ShapeDtypeStruct((64, 32, 128), BF16...  57.4 us

profile of v5, /device:TPU:1, one launch (start us, length us, event | category | flops | bytes accessed | tf_op | source)
XLA Modules:
  0.0 58.2 jit_solution(6669515187306548989)
XLA Ops:
  0.0 57.4 %triangle.1 = bf16[64,32,128]{2,1,0:T(8,128)(2,1)S(1)} custom-call(bf16[64,32,128]{2,1,0:T(8,128)(2,1)} %pair_hbm.1, f32[2,128]{1,0:T(2,128)} %ln_in_hbm.1, bf16[2,128,256]{2,1,0:T(8,128)(2,1)} %w_left_hbm.1, bf16[2,128,256]{2,1,0:T(8,128)(2,1)} %w_right_hbm.1, bf16[2,128,128]{2,1,0:T(8,128)(2,1)} %w_gate_hbm.1, f32[2,128]{1,0:T(2,128)} %ln_out_hbm.1, ...), custom_call_target="tpu_custom_call" | custom-call | tf_op jit(solution)/shard_map/triangle/pallas_call | solution.py:292
  57.4 0.8 %copy.9 = bf16[64,32,128]{2,1,0:T(8,128)(2,1)} copy(bf16[64,32,128]{2,1,0:T(8,128)(2,1)S(1)} %triangle.1) | data formatting | bytes 1048576

commit v6 on v5

--- a/solution.py
+++ b/solution.py
@@ -20,6 +20,9 @@
 
 
 ALL = sorted(itertools.product(range(4), range(4), range(4), range(2)), key=lambda d: (-hops(d), -d[3]))
+FAR = [d for d in ALL if hops(d) > 5]
+NEAR = [d for d in ALL if hops(d) <= 5]
+RELAYS = [(1, 0, 0, 0)]
 
 
 def norm_rows(values, gain):
@@ -48,7 +51,7 @@
     pair_ref, ln_in_ref, w_left_ref, w_right_ref, w_gate_ref, ln_out_ref, w_out_ref,
     flat, tile, normed, gate, spread_buf, w_proj, w_turn, right_t, left_rows,
     send_l, send_r, send_e, recv_l, recv_r, recv_e,
-    load_sem, send_sem, first_sem, second_sem, edge_sem,
+    load_sem, send_sem, first_sem, second_sem, edge_sem, ready,
 ):
     row, col = lax.axis_index("row"), lax.axis_index("col")
     x, y, z, core = row // 2, ((col // 2) % 2) * 2 + row % 2, col // 4, col % 2
@@ -82,7 +85,7 @@
         loads[-1].start()
 
     barrier = pltpu.get_barrier_semaphore()
-    for steps in ALL:
+    for steps in NEAR:
         if any(steps):
             pl.semaphore_signal(barrier, inc=1, device_id=device(steps), device_id_type=MESH)
 
@@ -136,20 +139,24 @@
         return carry
 
     lax.fori_loop(0, 4, project_all, 0)
-    pl.semaphore_wait(barrier, 127)
+    pl.semaphore_wait(barrier, len(NEAR) - 1)
+    for steps in RELAYS:
+        pl.semaphore_signal(ready, inc=1, device_id=device(steps), device_id_type=MESH)
 
     for u in range(2):
         slot = (row * 16 + col, core * 64 + row * 8 + col // 2)[u]
         side, send, recv = ((1, send_r, recv_r), (0, send_l, recv_l))[u]
 
+        first, first_recv = send, recv
+
         def send_first(steps):
             send_to(
-                send.at[u, at(channel(u, steps), 16), :], recv.at[u, at(slot, 16), :],
+                first.at[u, at(channel(u, steps), 16), :], first_recv.at[u, at(slot, 16), :],
                 send_sem.at[u, 0], first_sem.at[u, steps[3 * u]], steps,
             )
 
         if u == 0:
-            for steps in ALL:
+            for steps in NEAR:
                 send_first(steps)
         else:
             for dc, odd in OTHERS:
@@ -159,18 +166,31 @@
                         send_first(steps)
 
         side, send, recv = ((0, send_l, recv_l), (1, send_r, recv_r))[u]
-        if u == 0:
-            loads[3].wait()
-            prepare(0, 0)
-        for n, group in enumerate(GROUPS):
-            for k in range(2):
-                project(u, side, xs[group[k]] if u == 0 else cores[1 - n] * 2 + k, send)
-            for steps in ALL:
+        def send_second(n, some):
+            for steps in some:
                 if group_of(u, steps) == n:
                     send_to(
                         send.at[u, at(channel(u, steps), 16), :], recv.at[u, at(slot, 16), :],
                         send_sem.at[u, 1], second_sem.at[u, n], steps,
                     )
+
+        if u == 0:
+            loads[3].wait()
+            prepare(0, 0)
+            for k in range(2):
+                project(u, side, xs[GROUPS[0][k]], send)
+            pl.semaphore_wait(ready, len(RELAYS))
+            for steps in FAR:
+                send_first(steps)
+            send_second(0, ALL)
+            for k in range(2):
+                project(u, side, xs[GROUPS[1][k]], send)
+            send_second(1, ALL)
+        else:
+            for n in range(2):
+                for k in range(2):
+                    project(u, side, cores[1 - n] * 2 + k, send)
+                send_second(n, ALL)
 
         if u == 0:
             prepare(1, 0)
@@ -237,11 +257,11 @@
                 edges = lax.dot_general(
                     right, left_rows[...], (((1,), (1,)), ((), ())), preferred_element_type=F32
                 ).astype(BF16)
-                first, second = edges[:128], edges[128:]
+                top, bottom = edges[:128], edges[128:]
                 for k in range(8):
                     for m in range(4):
                         part = (slice(k * 16, k * 16 + 16), slice(m * 128, m * 128 + 128))
-                        low, high = swap_halves(first[part], second[part])
+                        low, high = swap_halves(top[part], bottom[part])
                         to = (n * 64 + k * 8 + 2 * m) * 16
                         send_e[u, to : to + 16, :] = low
                         send_e[u, to + 16 : to + 32, :] = high
@@ -311,6 +331,7 @@
             pltpu.SemaphoreType.DMA((2, 4)),
             pltpu.SemaphoreType.DMA((2, 2)),
             pltpu.SemaphoreType.DMA((2, 2)),
+            pltpu.SemaphoreType.REGULAR,
         ],
         compiler_params=pltpu.CompilerParams(
             collective_id=0, has_side_effects=True, vmem_limit_bytes=48 << 20

time: 58.5 us -> 57.3 us (0.979)
  Pallas kernels: 57.4 us -> 56.1 us
    pallas_call x1, Pallas kernels: 57.4 us -> 56.1 us  [local(): pl.pallas_call(kernel, out_shape=jax.ShapeDtypeStruct((64, 32, 128), BF16...]
where the time goes in v6:
time: 57.3 us; the launch traced here: 56.9 us
  Pallas kernels  56.1 us (98%)
  local copies, waits for them, and re-layouts  0.8 us (1%)
    pallas_call x1, Pallas kernels, local(): pl.pallas_call(kernel, out_shape=jax.ShapeDtypeStruct((64, 32, 128), BF16...  56.1 us

profile of v6, /device:TPU:1, one launch (start us, length us, event | category | flops | bytes accessed | tf_op | source)
XLA Modules:
  0.0 56.9 jit_solution(15510332661972760550)
XLA Ops:
  0.0 56.1 %triangle.1 = bf16[64,32,128]{2,1,0:T(8,128)(2,1)S(1)} custom-call(bf16[64,32,128]{2,1,0:T(8,128)(2,1)} %pair_hbm.1, f32[2,128]{1,0:T(2,128)} %ln_in_hbm.1, bf16[2,128,256]{2,1,0:T(8,128)(2,1)} %w_left_hbm.1, bf16[2,128,256]{2,1,0:T(8,128)(2,1)} %w_right_hbm.1, bf16[2,128,128]{2,1,0:T(8,128)(2,1)} %w_gate_hbm.1, f32[2,128]{1,0:T(2,128)} %ln_out_hbm.1, ...), custom_call_target="tpu_custom_call" | custom-call | tf_op jit(solution)/shard_map/triangle/pallas_call | solution.py:312
  56.1 0.8 %copy.9 = bf16[64,32,128]{2,1,0:T(8,128)(2,1)} copy(bf16[64,32,128]{2,1,0:T(8,128)(2,1)S(1)} %triangle.1) | data formatting | bytes 1048576

commit v7 on v6

--- a/solution.py
+++ b/solution.py
@@ -227,6 +227,19 @@
                                 c * 16 : c * 16 + 16
                             ]
 
+        def send_edges(n, some, place=0):
+            for steps in some:
+                if group_of(u, steps) == n:
+                    pr, pc = device(steps)
+                    if u == 0:
+                        there = (n * 2 + GROUPS[n].index(-steps[0] % 4)) * 32 + pr % 2 * 16 + place * 4 + pc % 4
+                    else:
+                        there = n * 64 + (pc // 2) * 8 + pr
+                    send_to(
+                        send_e.at[u, at(there, 16), :], recv_e.at[u, at(channel(u, (0, 0, 0, 0)), 16), :],
+                        send_sem.at[u, 2], edge_sem.at[u, n], steps,
+                    )
+
         for n, group in enumerate(GROUPS):
             if u == 0:
                 sources = [xs[-d % 4] for d in group]
@@ -237,16 +250,20 @@
                 left = jnp.concatenate(
                     [jnp.concatenate([pair[half] for pair in pairs], axis=1) for half in range(2)], axis=0
                 )
-                edges = jnp.dot(right_t[...], left, preferred_element_type=F32).astype(BF16)
-                for c in range(16):
-                    for k in range(2):
-                        lanes = slice(k * 128, k * 128 + 128)
-                        low, high = swap_halves(
-                            edges[c * 32 : c * 32 + 16, lanes], edges[c * 32 + 16 : c * 32 + 32, lanes]
-                        )
-                        to = (n * 64 + k * 32 + c) * 16
-                        send_e[u, to : to + 16, :] = low
-                        send_e[u, to + 256 : to + 272, :] = high
+                for place, dz in enumerate((2, 1, 3, 0)):
+                    edges = jnp.dot(
+                        right_t[at(zs[dz], 128), :], left, preferred_element_type=F32
+                    ).astype(BF16)
+                    for c in range(4):
+                        for k in range(2):
+                            lanes = slice(k * 128, k * 128 + 128)
+                            low, high = swap_halves(
+                                edges[c * 32 : c * 32 + 16, lanes], edges[c * 32 + 16 : c * 32 + 32, lanes]
+                            )
+                            to = (n * 64 + k * 32 + place * 4 + c) * 16
+                            send_e[u, to : to + 16, :] = low
+                            send_e[u, to + 256 : to + 272, :] = high
+                    send_edges(n, [steps for steps in ALL if steps[2] == dz], place)
             else:
                 arrived(recv_r, second_sem.at[u, n], 64)
                 g = cores[1 - n]
@@ -265,17 +282,7 @@
                         to = (n * 64 + k * 8 + 2 * m) * 16
                         send_e[u, to : to + 16, :] = low
                         send_e[u, to + 16 : to + 32, :] = high
-            for steps in ALL:
-                if group_of(u, steps) == n:
-                    pr, pc = device(steps)
-                    if u == 0:
-                        there = (n * 2 + group.index(-steps[0] % 4)) * 32 + pr % 2 * 16 + pc
-                    else:
-                        there = n * 64 + (pc // 2) * 8 + pr
-                    send_to(
-                        send_e.at[u, at(there, 16), :], recv_e.at[u, at(channel(u, (0, 0, 0, 0)), 16), :],
-                        send_sem.at[u, 2], edge_sem.at[u, n], steps,
-                    )
+                send_edges(n, ALL)
 
         gain_out = gain_of(ln_out_ref, u)
         gain_next = gain_of(ln_in_ref, 1)

time: 57.3 us -> 57.1 us (level)
  no operation moved by 1% of the time
where the time goes in v7:
time: 57.1 us; the launch traced here: 56.8 us
  Pallas kernels  56 us (98%)
  local copies, waits for them, and re-layouts  0.8 us (1%)
    pallas_call x1, Pallas kernels, local(): pl.pallas_call(kernel, out_shape=jax.ShapeDtypeStruct((64, 32, 128), BF16...  56 us

profile of v7, /device:TPU:1, one launch (start us, length us, event | category | flops | bytes accessed | tf_op | source)
XLA Modules:
  0.0 56.8 jit_solution(9479482610448066697)
XLA Ops:
  0.0 56.0 %triangle.1 = bf16[64,32,128]{2,1,0:T(8,128)(2,1)S(1)} custom-call(bf16[64,32,128]{2,1,0:T(8,128)(2,1)} %pair_hbm.1, f32[2,128]{1,0:T(2,128)} %ln_in_hbm.1, bf16[2,128,256]{2,1,0:T(8,128)(2,1)} %w_left_hbm.1, bf16[2,128,256]{2,1,0:T(8,128)(2,1)} %w_right_hbm.1, bf16[2,128,128]{2,1,0:T(8,128)(2,1)} %w_gate_hbm.1, f32[2,128]{1,0:T(2,128)} %ln_out_hbm.1, ...), custom_call_target="tpu_custom_call" | custom-call | tf_op jit(solution)/shard_map/triangle/pallas_call | solution.py:319
  56.0 0.8 %copy.9 = bf16[64,32,128]{2,1,0:T(8,128)(2,1)} copy(bf16[64,32,128]{2,1,0:T(8,128)(2,1)S(1)} %triangle.1) | data formatting | bytes 1048576
